TPU v7x, 32 devices: a whole 2x2x4 slice. The times are simulated.
32 devices in a mesh: groups: 2 (over x), enc: 16 (over z, y, core).
Axes of the slice: x: 2, y: 2, z: 4, core: 2. Of those that a mesh axis runs over, the one named last changes fastest.
Arguments:
- decoder_states: bfloat16 [128, 64, 768], P(('groups', 'enc')), parts along dimension 0, may hold values from -40 to 40
- cotangent: bfloat16 [128, 64, 768], P(('groups', 'enc')), parts along dimension 0, may hold values from -6 to 6
- encoded: bfloat16 [1024, 16, 768], P(('groups', 'enc')), parts along dimension 0, may hold values from -80 to 80
- valid_len: int32 [1024], P(('groups', 'enc')), parts along dimension 0, may hold values from 1 to 16
- retrieved: int32 [128, 16], P(('groups', 'enc')), parts along dimension 0, may hold values from 0 to 511, as said below
- w_query: bfloat16 [768, 768], replicated, may hold values from -0.21875 to 0.21875
- w_key: bfloat16 [768, 768], replicated, may hold values from -0.21875 to 0.21875
- w_value: bfloat16 [768, 768], replicated, may hold values from -0.21875 to 0.21875
- w_output: bfloat16 [768, 768], replicated, may hold values from -0.21875 to 0.21875
Outputs:
- attended: bfloat16 [128, 64, 768], P(('groups', 'enc')), parts along dimension 0
- d_decoder: bfloat16 [128, 64, 768], P(('groups', 'enc')), parts along dimension 0
- d_encoded: bfloat16 [1024, 16, 768], P(('groups', 'enc')), parts along dimension 0
- grad_query: float32 [1536, 768], P(('groups', 'enc')), parts along dimension 0
- grad_key: float32 [1536, 768], P(('groups', 'enc')), parts along dimension 0
- grad_value: float32 [1536, 768], P(('groups', 'enc')), parts along dimension 0
- grad_output: float32 [1536, 768], P(('groups', 'enc')), parts along dimension 0
There are 2 independent parts, one for each index of `groups`. A program takes and returns all parts, laid end to end along the dimension named above; an argument that names none is the same for every part. Nothing has to cross between parts.
Inputs may be any that keep to these rules, and one draw needn't show every extreme that they name: `retrieved`: passage p lives on device p // 32 of enc. Among the 64 ids of the questions of one device, no device owns more than 8; in each group one device owns exactly 8 of the ids of every device's questions. Ids may repeat within a question.
All inputs are finite; a program needn't handle non-finite values.
Results may differ from a plain program's by a relative error of at most 0.012.
The roundings to bfloat16 on the way count: a program that leaves them out, or rounds other values in their place, can miss the bound.
Values may be sent and summed in bfloat16 or wider, within the bound.
A program may use at most 128 MiB of HBM per device.

v0:
```python
import math

import jax
import jax.numpy as jnp
from jax import lax
from jax.sharding import PartitionSpec as P

HEADS = 12


def attend_core(queries, key_rows, value_rows, key_live, context_grad, score_scale):
    f32 = jnp.float32
    scores = (
        jnp.einsum("qthd,qshd->qhts", queries, key_rows, preferred_element_type=f32) * score_scale
    )
    scores = jnp.where(key_live[:, None, None, :], scores, -1e30)
    top = jnp.max(scores, axis=-1, keepdims=True)
    expo = jnp.exp(scores - top)
    probs = expo / jnp.sum(expo, axis=-1, keepdims=True)
    probs_b = probs.astype(jnp.bfloat16)
    context = jnp.einsum("qhts,qshd->qthd", probs_b, value_rows, preferred_element_type=f32).astype(
        jnp.bfloat16
    )
    prob_grad = jnp.einsum("qthd,qshd->qhts", context_grad, value_rows, preferred_element_type=f32)
    value_grad = jnp.einsum(
        "qhts,qthd->qshd", probs_b, context_grad, preferred_element_type=f32
    ).astype(jnp.bfloat16)
    inner = jnp.sum(probs * prob_grad, axis=-1, keepdims=True)
    score_grad = (probs * (prob_grad - inner) * score_scale).astype(jnp.bfloat16)
    query_grad = jnp.einsum(
        "qhts,qshd->qthd", score_grad, key_rows, preferred_element_type=f32
    ).astype(jnp.bfloat16)
    key_grad = jnp.einsum(
        "qhts,qthd->qshd", score_grad, queries, preferred_element_type=f32
    ).astype(jnp.bfloat16)
    return (context, query_grad, key_grad, value_grad)


def split_pair(summed):
    upper = summed.astype(jnp.bfloat16)
    lower = (summed - upper.astype(jnp.float32)).astype(jnp.bfloat16)
    return (upper, lower)


def body(
    decoder_states, cotangent, encoded, valid_len, retrieved, w_query, w_key, w_value, w_output
):
    f32 = jnp.float32
    devices = lax.axis_size("enc")
    questions_here, dec_len, model_width = decoder_states.shape
    passages_here, passage_len, _ = encoded.shape
    retrieved_per = retrieved.shape[1]
    slot_count = questions_here * retrieved_per
    capacity = max(2, 2 * slot_count // devices)
    head_dim = model_width // HEADS
    score_scale = 1.0 / math.sqrt(head_dim)
    flat_ids = retrieved.reshape(slot_count)
    owner_dev = flat_ids // passages_here
    local_idx = flat_ids % passages_here
    owner_hot = (owner_dev[:, None] == jnp.arange(devices, dtype=jnp.int32)[None, :]).astype(
        jnp.int32
    )
    earlier = jnp.cumsum(owner_hot, axis=0) - owner_hot
    slot_rank = jnp.sum(earlier * owner_hot, axis=1)
    position = owner_dev * capacity + slot_rank
    request = jnp.full((devices * capacity,), -1, jnp.int32).at[position].set(local_idx)
    incoming = lax.all_to_all(
        request.reshape(devices, capacity), "enc", split_axis=0, concat_axis=0, tiled=True
    )
    wanted = incoming.reshape(devices * capacity)
    is_live = wanted >= 0
    chosen_rows = jnp.where(is_live, wanted, 0)
    sent_len = (
        jnp.where(is_live, valid_len[chosen_rows], 0)
        .astype(jnp.bfloat16)
        .reshape(devices, capacity)
    )
    enc_flat = encoded.reshape(passages_here * passage_len, model_width)
    send_shape = (devices, capacity, passage_len, model_width)
    slot_shape = (devices * capacity, passage_len, model_width)
    key_table = (
        jnp.dot(enc_flat, w_key, preferred_element_type=f32)
        .astype(jnp.bfloat16)
        .reshape(passages_here, passage_len, model_width)
    )
    value_table = (
        jnp.dot(enc_flat, w_value, preferred_element_type=f32)
        .astype(jnp.bfloat16)
        .reshape(passages_here, passage_len, model_width)
    )
    got_keys, got_values, got_len = (
        lax.all_to_all(
            key_table[chosen_rows].reshape(send_shape),
            "enc",
            split_axis=0,
            concat_axis=0,
            tiled=True,
        ),
        lax.all_to_all(
            value_table[chosen_rows].reshape(send_shape),
            "enc",
            split_axis=0,
            concat_axis=0,
            tiled=True,
        ),
        lax.all_to_all(sent_len, "enc", split_axis=0, concat_axis=0, tiled=True),
    )
    slot_keys = got_keys.reshape(slot_shape)[position]
    slot_values = got_values.reshape(slot_shape)[position]
    slot_len = got_len.reshape(devices * capacity)[position].astype(f32)
    token_pos = jnp.arange(passage_len, dtype=jnp.int32).astype(f32)
    key_live = (token_pos[None, :] < slot_len[:, None]).reshape(
        questions_here, retrieved_per * passage_len
    )
    dec_flat = decoder_states.reshape(questions_here * dec_len, model_width)
    cot_flat = cotangent.reshape(questions_here * dec_len, model_width)
    head_shape = (questions_here, dec_len, HEADS, head_dim)
    kv_shape = (questions_here, retrieved_per * passage_len, HEADS, head_dim)
    queries = (
        jnp.dot(dec_flat, w_query, preferred_element_type=f32)
        .astype(jnp.bfloat16)
        .reshape(head_shape)
    )
    context_grad = (
        jnp.dot(cot_flat, w_output.T, preferred_element_type=f32)
        .astype(jnp.bfloat16)
        .reshape(head_shape)
    )
    context, query_grad, key_grad, value_grad = attend_core(
        queries,
        slot_keys.reshape(kv_shape),
        slot_values.reshape(kv_shape),
        key_live,
        context_grad,
        score_scale,
    )
    ctx_flat = context.reshape(questions_here * dec_len, model_width)
    attended = jnp.dot(ctx_flat, w_output, preferred_element_type=f32).astype(jnp.bfloat16)
    grad_out_part = jnp.dot(ctx_flat.T, cot_flat, preferred_element_type=f32)
    qg_flat = query_grad.reshape(questions_here * dec_len, model_width)
    d_decoder = jnp.dot(qg_flat, w_query.T, preferred_element_type=f32).astype(jnp.bfloat16)
    grad_q_part = jnp.dot(dec_flat.T, qg_flat, preferred_element_type=f32)
    kg_rows = key_grad.reshape(slot_count * passage_len, model_width)
    vg_rows = value_grad.reshape(slot_count * passage_len, model_width)
    out_keys = (
        jnp.zeros(slot_shape, jnp.bfloat16)
        .at[position]
        .set(kg_rows.reshape(slot_count, passage_len, model_width))
        .reshape(send_shape)
    )
    out_values = (
        jnp.zeros(slot_shape, jnp.bfloat16)
        .at[position]
        .set(vg_rows.reshape(slot_count, passage_len, model_width))
        .reshape(send_shape)
    )
    ret_keys, ret_values = (
        lax.all_to_all(out_keys, "enc", split_axis=0, concat_axis=0, tiled=True),
        lax.all_to_all(out_values, "enc", split_axis=0, concat_axis=0, tiled=True),
    )
    select_b = (jnp.arange(passages_here, dtype=jnp.int32)[:, None] == wanted[None, :]).astype(
        jnp.bfloat16
    )
    summed_keys = jnp.dot(
        select_b,
        ret_keys.reshape(devices * capacity, passage_len * model_width),
        preferred_element_type=f32,
    ).reshape(passages_here * passage_len, model_width)
    summed_values = jnp.dot(
        select_b,
        ret_values.reshape(devices * capacity, passage_len * model_width),
        preferred_element_type=f32,
    ).reshape(passages_here * passage_len, model_width)
    key_upper, key_lower = split_pair(summed_keys)
    value_upper, value_lower = split_pair(summed_values)
    stacked = jnp.concatenate([key_upper, key_lower, value_upper, value_lower], axis=1)
    back_weights = jnp.concatenate([w_key.T, w_key.T, w_value.T, w_value.T], axis=0)
    d_encoded = jnp.dot(stacked, back_weights, preferred_element_type=f32).astype(jnp.bfloat16)
    weight_terms = jnp.einsum("rd,re->de", enc_flat, stacked, preferred_element_type=f32)
    grad_k_part = weight_terms[:, :model_width] + weight_terms[:, model_width : 2 * model_width]
    grad_v_part = (
        weight_terms[:, 2 * model_width : 3 * model_width] + weight_terms[:, 3 * model_width :]
    )
    weight_grads = (
        lax.psum_scatter(grad_q_part, "enc", scatter_dimension=0, tiled=True),
        lax.psum_scatter(grad_k_part, "enc", scatter_dimension=0, tiled=True),
        lax.psum_scatter(grad_v_part, "enc", scatter_dimension=0, tiled=True),
        lax.psum_scatter(grad_out_part, "enc", scatter_dimension=0, tiled=True),
    )
    return (
        attended.reshape(decoder_states.shape),
        d_decoder.reshape(decoder_states.shape),
        d_encoded.reshape(encoded.shape),
        weight_grads[0],
        weight_grads[1],
        weight_grads[2],
        weight_grads[3],
    )


def solution(mesh):
    in_specs = (
        P(("groups", "enc"), None, None),
        P(("groups", "enc"), None, None),
        P(("groups", "enc"), None, None),
        P(("groups", "enc")),
        P(("groups", "enc"), None),
        P(),
        P(),
        P(),
        P(),
    )
    out_specs = (
        P(("groups", "enc"), None, None),
        P(("groups", "enc"), None, None),
        P(("groups", "enc"), None, None),
        P(("groups", "enc"), None),
        P(("groups", "enc"), None),
        P(("groups", "enc"), None),
        P(("groups", "enc"), None),
    )
    return jax.shard_map(body, mesh=mesh, in_specs=in_specs, out_specs=out_specs, check_vma=False)
```

profile of v0, /device:TPU:0, one launch (start us, length us, event | category | flops | bytes accessed | tf_op | source)
XLA Modules:
  0.0 637.7 jit_solution(4577794398199852613)
XLA Ops:
  10.6 13.6 %all_to_all.35 = s32[16,1,8]{2,1,0:T(1,128)S(1)} all-to-all(s32[16,1,8]{2,1,0:T(1,128)S(1)} %bitcast.94), channel_id=1, replica_groups=mesh['groups'=2,'enc'=16] {'enc'}, dimensions={0} | all-to-all | bytes 1024 | tf_op jit(solution)/shard_map/all_to_all | solution.py:67
  46.8 55.0 %all-to-all-done.1 = bf16[16,8,16,768]{3,2,1,0:T(8,128)(2,1)} async-done(((bf16[16,8,16,768]{3,2,1,0:T(8,128)(2,1)}), bf16[16,8,16,768]{3,2,1,0:T(8,128)(2,1)}, u32[]{:S(2)}, u32[]{:S(2)}) %all-to-all-start.1) | async-done | bytes 3145760 | tf_op jit(solution)/shard_map/all_to_all | solution.py:99
  101.8 15.8 %all-to-all-start.3 = ((bf16[16,8,16,768]{3,2,1,0:T(8,128)(2,1)}), bf16[16,8,16,768]{3,2,1,0:T(8,128)(2,1)}, u32[]{:S(2)}, u32[]{:S(2)}) async-start(bf16[16,8,16,768]{3,2,1,0:T(8,128)(2,1)} %bitcast.82), calls=%async_computation.3 | async-start | bytes 6291456 | tf_op jit(solution)/shard_map/all_to_all | solution.py:92
  135.1 41.9 %all-to-all-done.3 = bf16[16,8,16,768]{3,2,1,0:T(8,128)(2,1)} async-done(((bf16[16,8,16,768]{3,2,1,0:T(8,128)(2,1)}), bf16[16,8,16,768]{3,2,1,0:T(8,128)(2,1)}, u32[]{:S(2)}, u32[]{:S(2)}) %all-to-all-start.3) | async-done | bytes 3145760 | tf_op jit(solution)/shard_map/all_to_all | solution.py:92
  180.9 5.9 reshape.280
  186.8 5.3 copy.66
  194.3 5.0 fusion.65
  199.3 21.9 %fusion.28 = bf16[4,256,12,64]{1,3,2,0:T(8,128)(2,1)S(1)} fusion(bf16[4,64,12,64]{1,3,2,0:T(8,128)(2,1)} %copy.74, f32[4,12,64,256]{3,2,1,0:T(8,128)} %fusion.66, f32[4,12,64,256]{3,2,1,0:T(8,128)} %get-tuple-element.44, f32[4,12,64]{2,1,0:T(8,128)} %get-tuple-element.43), kind=kOutput, calls=%fused_computation.42 | convolution fusion | flops 106958080 | bytes 8269824 | tf_op jit(solution)/shard_map/qhts,qthd->qshd/dot_general | solution.py:33
  221.2 5.0 copy.75
  226.2 5.2 reshape.355
  233.3 8.4 %scatter_fusion = bf16[128,16,768]{2,1,0:T(8,128)(2,1)} fusion(bf16[128,16,768]{2,1,0:T(8,128)(2,1)} %broadcast.168.clone, s32[64]{0:T(128)S(1)} %copy-done.21, bf16[64,16,768]{2,1,0:T(8,128)(2,1)S(1)} %reshape.355), kind=kCustom, calls=%fused_computation.7 | custom fusion | bytes 4718848 | tf_op jit(solution)/shard_map/scatter | solution.py:148
  241.7 15.4 %all-to-all-start.4 = ((bf16[16,8,16,768]{3,2,1,0:T(8,128)(2,1)}), bf16[16,8,16,768]{3,2,1,0:T(8,128)(2,1)}, u32[]{:S(2)}, u32[]{:S(2)}) async-start(bf16[16,8,16,768]{3,2,1,0:T(8,128)(2,1)} %bitcast.81), calls=%async_computation.4 | async-start | bytes 6291456 | tf_op jit(solution)/shard_map/all_to_all | solution.py:158
  259.7 4.8 copy.77
  264.4 5.2 reshape.363
  271.5 8.4 %scatter_fusion.1 = bf16[128,16,768]{2,1,0:T(8,128)(2,1)} fusion(bf16[128,16,768]{2,1,0:T(8,128)(2,1)} %broadcast.168.clone.1, s32[64]{0:T(128)S(1)} %copy-done.21, bf16[64,16,768]{2,1,0:T(8,128)(2,1)S(1)} %reshape.363), kind=kCustom, calls=%fused_computation.8 | custom fusion | bytes 4718848 | tf_op jit(solution)/shard_map/scatter | solution.py:154
  279.9 36.7 %all-to-all-done.4 = bf16[16,8,16,768]{3,2,1,0:T(8,128)(2,1)} async-done(((bf16[16,8,16,768]{3,2,1,0:T(8,128)(2,1)}), bf16[16,8,16,768]{3,2,1,0:T(8,128)(2,1)}, u32[]{:S(2)}, u32[]{:S(2)}) %all-to-all-start.4) | async-done | bytes 3145760 | tf_op jit(solution)/shard_map/all_to_all | solution.py:158
  316.5 15.6 %all-to-all-start.5 = ((bf16[16,8,16,768]{3,2,1,0:T(8,128)(2,1)}), bf16[16,8,16,768]{3,2,1,0:T(8,128)(2,1)}, u32[]{:S(2)}, u32[]{:S(2)}) async-start(bf16[16,8,16,768]{3,2,1,0:T(8,128)(2,1)} %bitcast.80), calls=%async_computation.5 | async-start | bytes 6291456 | tf_op jit(solution)/shard_map/all_to_all | solution.py:159
  332.2 21.4 %fusion.39 = bf16[4,64,12,64]{1,3,2,0:T(8,128)(2,1)S(1)} fusion(bf16[4,256,12,64]{1,3,2,0:T(8,128)(2,1)S(1)} %copy-done.6, f32[4,12,64,256]{3,2,1,0:T(8,128)} %fusion.66, f32[4,12,64,256]{3,2,1,0:T(8,128)} %get-tuple-element.44, f32[4,12,64]{2,1,0:T(8,128)} %get-tuple-element.43), kind=kOutput, calls=%fused_computation.50 | convolution fusion | flops 106368256 | bytes 8269824 | tf_op jit(solution)/shard_map/qhts,qshd->qthd/dot_general | solution.py:30
  370.9 20.8 %all-to-all-done.5 = bf16[16,8,16,768]{3,2,1,0:T(8,128)(2,1)} async-done(((bf16[16,8,16,768]{3,2,1,0:T(8,128)(2,1)}), bf16[16,8,16,768]{3,2,1,0:T(8,128)(2,1)}, u32[]{:S(2)}, u32[]{:S(2)}) %all-to-all-start.5) | async-done | bytes 3145760 | tf_op jit(solution)/shard_map/all_to_all | solution.py:159
  415.5 5.2 fusion.35
  420.7 10.3 %reduce-scatter.13.cloned.1.call-done = f32[48,768]{1,0:T(8,128)} async-done(((f32[768,768]{1,0:T(8,128)}), f32[48,768]{1,0:T(8,128)}) %reduce-scatter.13.cloned.1.call-update) | async-done | bytes 147472
  431.0 66.8 %reduce-scatter.11.cloned.1.call-done = f32[48,768]{1,0:T(8,128)} async-done(((f32[768,768]{1,0:T(8,128)}), f32[48,768]{1,0:T(8,128)}) %reduce-scatter.11.cloned.1.call-update) | async-done | bytes 147472 | tf_op jit(solution)/shard_map/reduce_scatter | solution.py:188
  497.8 66.3 %reduce-scatter.15.cloned.1.call-done = f32[48,768]{1,0:T(8,128)} async-done(((f32[768,768]{1,0:T(8,128)}), f32[48,768]{1,0:T(8,128)}) %reduce-scatter.15.cloned.1.call-update) | async-done | bytes 147472
  564.1 66.7 %reduce-scatter.17.cloned.1.call-done = f32[48,768]{1,0:T(8,128)} async-done(((f32[768,768]{1,0:T(8,128)}), f32[48,768]{1,0:T(8,128)}) %reduce-scatter.17.cloned.1.call-update) | async-done | bytes 147472
  (134 shorter events, 96.6 us)
Async XLA Ops:
  7.2 113.8 %copy-start = (bf16[768,768]{1,0:T(8,128)(2,1)S(1)}, bf16[768,768]{1,0:T(8,128)(2,1)}, u32[]{:S(2)}) copy-start(bf16[768,768]{1,0:T(8,128)(2,1)} %param.17) | copy-start | bytes 3538948
  28.0 9.8 %all-to-all-start.2 = ((bf16[16,1,8]{2,1,0:T(2,128)(2,1)}), bf16[16,1,8]{2,1,0:T(2,128)(2,1)S(1)}, u32[]{:S(2)}, u32[]{:S(2)}) async-start(bf16[16,1,8]{2,1,0:T(2,128)(2,1)} %copy.63), calls=%async_computation.2 | async-start | bytes 16384 | tf_op jit(solution)/shard_map/all_to_all | solution.py:106
  37.8 4.6 copy-start.24
  37.8 64.0 %all-to-all-start.1 = ((bf16[16,8,16,768]{3,2,1,0:T(8,128)(2,1)}), bf16[16,8,16,768]{3,2,1,0:T(8,128)(2,1)}, u32[]{:S(2)}, u32[]{:S(2)}) async-start(bf16[16,8,16,768]{3,2,1,0:T(8,128)(2,1)} %bitcast.83), calls=%async_computation.1 | async-start | bytes 6291456 | tf_op jit(solution)/shard_map/all_to_all | solution.py:99
  101.8 16.5 %copy-start.2 = (bf16[768,768]{1,0:T(8,128)(2,1)S(1)}, bf16[768,768]{1,0:T(8,128)(2,1)}, u32[]{:S(2)}) copy-start(bf16[768,768]{1,0:T(8,128)(2,1)} %param.14) | copy-start | bytes 3538948
  101.8 16.5 %copy-start.7 = (bf16[4,64,768]{2,1,0:T(8,128)(2,1)S(1)}, bf16[4,64,768]{2,1,0:T(8,128)(2,1)}, u32[]{:S(2)}) copy-start(bf16[4,64,768]{2,1,0:T(8,128)(2,1)} %param.9) | copy-start | bytes 1179652
  101.8 75.2 %all-to-all-start.3 = ((bf16[16,8,16,768]{3,2,1,0:T(8,128)(2,1)}), bf16[16,8,16,768]{3,2,1,0:T(8,128)(2,1)}, u32[]{:S(2)}, u32[]{:S(2)}) async-start(bf16[16,8,16,768]{3,2,1,0:T(8,128)(2,1)} %bitcast.82), calls=%async_computation.3 | async-start | bytes 6291456 | tf_op jit(solution)/shard_map/all_to_all | solution.py:92
  135.1 56.9 %copy-start.1 = (bf16[4,256,12,64]{1,3,2,0:T(8,128)(2,1)}, bf16[4,256,12,64]{1,3,2,0:T(8,128)(2,1)S(1)}, u32[]{:S(2)}) copy-start(bf16[4,256,12,64]{1,3,2,0:T(8,128)(2,1)S(1)} %copy.67) | copy-start | bytes 4718596
  226.2 7.1 %copy-start.21 = (s32[64]{0:T(128)S(1)}, s32[64]{0:T(128)}, u32[]{:S(2)}) copy-start(s32[64]{0:T(128)} %copy-done.19) | copy-start | bytes 772
  241.7 74.9 %all-to-all-start.4 = ((bf16[16,8,16,768]{3,2,1,0:T(8,128)(2,1)}), bf16[16,8,16,768]{3,2,1,0:T(8,128)(2,1)}, u32[]{:S(2)}, u32[]{:S(2)}) async-start(bf16[16,8,16,768]{3,2,1,0:T(8,128)(2,1)} %bitcast.81), calls=%async_computation.4 | async-start | bytes 6291456 | tf_op jit(solution)/shard_map/all_to_all | solution.py:158
  316.5 15.7 %copy-start.6 = (bf16[4,256,12,64]{1,3,2,0:T(8,128)(2,1)S(1)}, bf16[4,256,12,64]{1,3,2,0:T(8,128)(2,1)}, u32[]{:S(2)}) copy-start(bf16[4,256,12,64]{1,3,2,0:T(8,128)(2,1)} %copy.66) | copy-start | bytes 4718596
  316.5 75.1 %all-to-all-start.5 = ((bf16[16,8,16,768]{3,2,1,0:T(8,128)(2,1)}), bf16[16,8,16,768]{3,2,1,0:T(8,128)(2,1)}, u32[]{:S(2)}, u32[]{:S(2)}) async-start(bf16[16,8,16,768]{3,2,1,0:T(8,128)(2,1)} %bitcast.80), calls=%async_computation.5 | async-start | bytes 6291456 | tf_op jit(solution)/shard_map/all_to_all | solution.py:159
  332.2 98.8 %reduce-scatter.13.cloned.1.call-start = ((), (), s32[]{:S(2)}) async-start(), calls=%async_computation.11 | async-start | bytes 2506752
  359.2 4.2 copy-start.9
  359.2 138.6 %reduce-scatter.11.cloned.1.call-start = ((), (), s32[]{:S(2)}) async-start(), calls=%async_computation.10 | async-start | bytes 2506752 | tf_op jit(solution)/shard_map/reduce_scatter | solution.py:188
  363.4 5.5 copy-start.5
  365.4 198.7 %reduce-scatter.15.cloned.1.call-start = ((), (), s32[]{:S(2)}) async-start(), calls=%async_computation.12 | async-start | bytes 2506752
  396.7 5.2 copy-start.25
  409.7 221.1 %reduce-scatter.17.cloned.1.call-start = ((), (), s32[]{:S(2)}) async-start(), calls=%async_computation.13 | async-start | bytes 2506752
  411.7 3.7 copy-start.11
  411.7 3.7 copy-start.13
  411.7 3.7 copy-start.15
  411.8 3.7 copy-start.17
  411.8 3.7 copy-start.23
  (11 other events, 21.7 us)
Sparse Core Ops, SparseCore 0:
  359.3 71.6 reduce-scatter.12
  435.8 61.9 reduce-scatter.10
  502.1 61.9 reduce-scatter.14
  568.8 61.9 reduce-scatter.16
where the time goes:
time: 643 us; the launch traced here: 638 us
  waiting for transfers between devices  366 us (57%)
  local copies, waits for them, and re-layouts  104 us (16%)
  matrix products  77.6 us (12%)
  starting transfers between devices  55.3 us (9%)
  between operations  14.7 us (2%)
  blocking collectives  13.6 us (2%)
  other arithmetic  6.59 us (1%)
    unnamed x7, waiting for transfers between devices  143 us
    reduce_scatter x1, waiting for transfers between devices, body(): lax.psum_scatter(grad_out_part, 'enc', scatter_dimension=0, tiled=True)  66.8 us
    all_to_all x1, waiting for transfers between devices, body(): lax.all_to_all(value_table[chosen_rows].reshape(send_shape), 'enc', split...  55 us
    all_to_all x1, waiting for transfers between devices, body(): lax.all_to_all(key_table[chosen_rows].reshape(send_shape), 'enc', split_a...  41.9 us
    all_to_all x1, waiting for transfers between devices, body(): lax.all_to_all(out_keys, 'enc', split_axis=0, concat_axis=0, tiled=True)  36.7 us
    dot_general x1, matrix products, attend_core(): jnp.einsum('qhts,qthd->qshd', score_grad, queries, preferred_element_type...  21.9 us
    dot_general x1, matrix products, attend_core(): jnp.einsum('qhts,qshd->qthd', score_grad, key_rows, preferred_element_typ...  21.4 us
    all_to_all x1, waiting for transfers between devices, body(): lax.all_to_all(out_values, 'enc', split_axis=0, concat_axis=0, tiled=True)  20.8 us
  transfers between devices with their start and end apart: 9, of which 9 were waited for; matrix products, arithmetic and copies ran while one was open for 18% of the time, Pallas kernels for 0%

commit v1 on v0

v1 whole, which is shorter than its diff:
```python
import functools
import math

import jax
import jax.numpy as jnp
from jax import lax
from jax.experimental import pallas as pl
from jax.experimental.pallas import tpu as pltpu
from jax.sharding import PartitionSpec as P

HEADS = 12
MESH = pl.DeviceIdType.MESH
BF = jnp.bfloat16
F32 = jnp.float32


def place(me):
    return me // 4, (me // 2) % 2, me % 2


def index_of(z, y, c):
    return z * 4 + y * 2 + c


def greet_all(n, me):
    barrier = pltpu.get_barrier_semaphore()
    for k in range(1, n):
        pl.semaphore_signal(
            barrier, inc=1, device_id={"enc": lax.rem(me + k, n)}, device_id_type=MESH
        )
    pl.semaphore_wait(barrier, n - 1)


def gather_kernel(
    n, cut, enc_ref, info_ref, table_ref, infos_ref, send_sem, recv_sem, info_send, info_recv, own_sem
):
    depth = n // 4
    me = lax.axis_index("enc")
    z, y, c = place(me)
    rows = enc_ref.shape[0]
    spans = (pl.ds(0, cut), pl.ds(cut, rows - cut))
    greet_all(n, me)

    owns = [pltpu.make_async_copy(enc_ref, table_ref.at[me], own_sem.at[0])]
    owns.append(pltpu.make_async_copy(info_ref, infos_ref.at[me], own_sem.at[1]))
    sends = []

    def send(cond, src, origin, half, kind, target):
        copy = pltpu.make_async_remote_copy(
            src_ref=src,
            dst_ref=table_ref.at[origin, spans[half]],
            send_sem=send_sem.at[kind, half, origin],
            recv_sem=recv_sem.at[half, origin],
            device_id={"enc": target},
            device_id_type=MESH,
        )
        sends.append((cond, copy))
        if cond is None:
            copy.start()
        else:
            pl.when(cond)(copy.start)

    def arrive(cond, origin, half):
        copy = pltpu.make_async_remote_copy(
            src_ref=table_ref.at[origin, spans[half]],
            dst_ref=table_ref.at[origin, spans[half]],
            send_sem=send_sem.at[0, half, origin],
            recv_sem=recv_sem.at[half, origin],
            device_id={"enc": me},
            device_id_type=MESH,
        )
        if cond is None:
            copy.wait_recv()
        else:
            pl.when(cond)(copy.wait_recv)

    up_ok, down_ok = z < depth - 1, z > 0
    up = index_of(jnp.minimum(z + 1, depth - 1), y, c)
    down = index_of(jnp.maximum(z - 1, 0), y, c)
    across = index_of(z, 1 - y, c)
    sibling = index_of(z, y, 1 - c)

    own = [enc_ref.at[span] for span in spans]
    send(None, own[1], me, 1, 2, across)
    send(up_ok, own[0], me, 0, 0, up)
    send(down_ok, own[0], me, 0, 1, down)
    send(None, own[0], me, 0, 2, across)
    send(up_ok, own[1], me, 1, 0, up)
    send(down_ok, own[1], me, 1, 1, down)
    for half in range(2):
        send(None, own[half], me, half, 3, sibling)
    info_copies = []
    for k in range(1, n):
        copy = pltpu.make_async_remote_copy(
            src_ref=info_ref,
            dst_ref=infos_ref.at[me],
            send_sem=info_send.at[k],
            recv_sem=info_recv.at[me],
            device_id={"enc": lax.rem(me + k, n)},
            device_id_type=MESH,
        )
        copy.start()
        info_copies.append(copy)
    for copy in owns:
        copy.start()

    def passed(cond, origin, half, go_up, go_down, go_across):
        arrive(cond, origin, half)
        block = table_ref.at[origin, spans[half]]
        both = lambda a: a if cond is None else jnp.logical_and(cond, a)
        if go_up:
            send(both(up_ok), block, origin, half, 0, up)
        if go_down:
            send(both(down_ok), block, origin, half, 1, down)
        if go_across:
            send(cond, block, origin, half, 2, across)
        send(cond, block, origin, half, 3, sibling)

    passed(None, across, 1, True, True, False)
    for d in range(1, depth):
        for sign in (1, -1):
            zo = z - sign * d
            cond = jnp.logical_and(zo >= 0, zo < depth)
            zc = jnp.clip(zo, 0, depth - 1)
            passed(cond, index_of(zc, y, c), 0, sign > 0, sign < 0, True)
            passed(cond, index_of(zc, y, c), 1, sign > 0, sign < 0, False)
            passed(cond, index_of(zc, 1 - y, c), 1, sign > 0, sign < 0, False)
        if d == 1:
            passed(None, across, 0, False, False, False)
        for sign in (1, -1):
            zo = z - sign * d
            cond = jnp.logical_and(zo >= 0, zo < depth)
            zc = jnp.clip(zo, 0, depth - 1)
            passed(cond, index_of(zc, 1 - y, c), 0, False, False, False)
    for zo in range(depth):
        for yo in range(2):
            for half in range(2):
                arrive(None, index_of(zo, yo, 1 - c), half)
    for cond, copy in sends:
        if cond is None:
            copy.wait_send()
        else:
            pl.when(cond)(copy.wait_send)
    for k in range(1, n):
        info_copies[k - 1].wait_send()
        source = lax.rem(me + n - k, n)
        pltpu.make_async_remote_copy(
            src_ref=info_ref,
            dst_ref=infos_ref.at[source],
            send_sem=info_send.at[k],
            recv_sem=info_recv.at[source],
            device_id={"enc": source},
            device_id_type=MESH,
        ).wait_recv()
    for copy in owns:
        copy.wait()


def gather_all(encoded_flat, info, n):
    rows, width = encoded_flat.shape
    cut = rows * 13 // 16 // 16 * 16
    hbm = pl.BlockSpec(memory_space=pl.ANY)
    return pl.pallas_call(
        functools.partial(gather_kernel, n, cut),
        out_shape=(
            jax.ShapeDtypeStruct((n, rows, width), BF),
            jax.ShapeDtypeStruct((n,) + info.shape, jnp.int32),
        ),
        in_specs=[hbm, hbm],
        out_specs=(hbm, hbm),
        scratch_shapes=[
            pltpu.SemaphoreType.DMA((4, 2, n)),
            pltpu.SemaphoreType.DMA((2, n)),
            pltpu.SemaphoreType.DMA((n,)),
            pltpu.SemaphoreType.DMA((n,)),
            pltpu.SemaphoreType.DMA((2,)),
        ],
        compiler_params=pltpu.CompilerParams(collective_id=0, has_side_effects=True),
        name="gather_passages",
    )(encoded_flat, info)


def return_kernel(
    n, slots_ref, g_ref, got_ref, gout_ref, r1, s1, r2, s2, r3, sem1, sem2, send3, recv3, send_a, recv_a, own_sem
):
    depth = n // 4
    me = lax.axis_index("enc")
    z, y, c = place(me)
    sibling = index_of(z, y, 1 - c)
    across = index_of(z, 1 - y, c)
    greet_all(n, me)

    def remote(src, dst, ssem, rsem, target):
        return pltpu.make_async_remote_copy(
            src_ref=src, dst_ref=dst, send_sem=ssem, recv_sem=rsem,
            device_id={"enc": target}, device_id_type=MESH,
        )

    first = remote(g_ref.at[1 - c], r1, sem1.at[0], sem1.at[1], sibling)
    first.start()
    slot_copies = []
    for k in range(1, n):
        target = lax.rem(me + k, n)
        copy = remote(slots_ref.at[target], got_ref.at[me], send_a.at[k], recv_a.at[me], target)
        copy.start()
        slot_copies.append(copy)
    own = pltpu.make_async_copy(slots_ref.at[me], got_ref.at[me], own_sem)
    own.start()
    first.wait()

    def add1(i, carry):
        for yy in range(2):
            s1[yy, i] = (g_ref[c, yy, i].astype(F32) + r1[yy, i].astype(F32)).astype(BF)
        return carry

    lax.fori_loop(0, depth, add1, 0)
    second = remote(s1.at[1 - y], r2, sem2.at[0], sem2.at[1], across)
    second.start()
    second.wait()

    def add2(i, carry):
        s2[i] = (s1[y, i].astype(F32) + r2[i].astype(F32)).astype(BF)
        return carry

    lax.fori_loop(0, depth, add2, 0)
    thirds = []
    for k in range(1, depth):
        zt = lax.rem(z + k, depth)
        copy = remote(s2.at[zt], r3.at[z], send3.at[k], recv3.at[z], index_of(zt, y, c))
        copy.start()
        thirds.append(copy)
    for k in range(1, depth):
        thirds[k - 1].wait_send()
        zs = lax.rem(z + depth - k, depth)
        remote(s2.at[zs], r3.at[zs], send3.at[k], recv3.at[zs], index_of(zs, y, c)).wait_recv()
    gout_ref[...] = s2[z].astype(F32)
    for k in range(1, depth):
        gout_ref[...] += r3[lax.rem(z + k, depth)].astype(F32)
    for k in range(1, n):
        slot_copies[k - 1].wait_send()
        source = lax.rem(me + n - k, n)
        remote(slots_ref.at[source], got_ref.at[source], send_a.at[k], recv_a.at[source], source).wait_recv()
    own.wait()


def return_all(slots, grads, n):
    depth = n // 4
    high, width = grads.shape[-2:]
    hbm = pl.BlockSpec(memory_space=pl.ANY)
    vmem = pl.BlockSpec(memory_space=pltpu.VMEM)
    return pl.pallas_call(
        functools.partial(return_kernel, n),
        out_shape=(
            jax.ShapeDtypeStruct(slots.shape, BF),
            jax.ShapeDtypeStruct((high, width), F32),
        ),
        in_specs=[hbm, vmem],
        out_specs=(hbm, vmem),
        scratch_shapes=[
            pltpu.VMEM((2, depth, high, width), BF),
            pltpu.VMEM((2, depth, high, width), BF),
            pltpu.VMEM((depth, high, width), BF),
            pltpu.VMEM((depth, high, width), BF),
            pltpu.VMEM((depth, high, width), BF),
            pltpu.SemaphoreType.DMA((2,)),
            pltpu.SemaphoreType.DMA((2,)),
            pltpu.SemaphoreType.DMA((depth,)),
            pltpu.SemaphoreType.DMA((depth,)),
            pltpu.SemaphoreType.DMA((n,)),
            pltpu.SemaphoreType.DMA((n,)),
            pltpu.SemaphoreType.DMA(()),
        ],
        compiler_params=pltpu.CompilerParams(
            collective_id=1, has_side_effects=True, vmem_limit_bytes=48 * 2**20
        ),
        name="return_gradients",
    )(slots, grads)


def attend_core(queries, key_rows, value_rows, key_live, context_grad, score_scale):
    scores = (
        jnp.einsum("qthd,qshd->qhts", queries, key_rows, preferred_element_type=F32) * score_scale
    )
    scores = jnp.where(key_live[:, None, None, :], scores, -1e30)
    top = jnp.max(scores, axis=-1, keepdims=True)
    expo = jnp.exp(scores - top)
    probs = expo / jnp.sum(expo, axis=-1, keepdims=True)
    probs_b = probs.astype(BF)
    context = jnp.einsum("qhts,qshd->qthd", probs_b, value_rows, preferred_element_type=F32).astype(BF)
    prob_grad = jnp.einsum("qthd,qshd->qhts", context_grad, value_rows, preferred_element_type=F32)
    value_grad = jnp.einsum("qhts,qthd->qshd", probs_b, context_grad, preferred_element_type=F32).astype(BF)
    inner = jnp.sum(probs * prob_grad, axis=-1, keepdims=True)
    score_grad = (probs * (prob_grad - inner) * score_scale).astype(BF)
    query_grad = jnp.einsum("qhts,qshd->qthd", score_grad, key_rows, preferred_element_type=F32).astype(BF)
    key_grad = jnp.einsum("qhts,qthd->qshd", score_grad, queries, preferred_element_type=F32).astype(BF)
    return (context, query_grad, key_grad, value_grad)


def body(
    decoder_states, cotangent, encoded, valid_len, retrieved, w_query, w_key, w_value, w_output
):
    n = lax.axis_size("enc")
    me = lax.axis_index("enc")
    questions_here, dec_len, width = decoder_states.shape
    passages_here, passage_len, _ = encoded.shape
    per_question = retrieved.shape[1]
    slot_count = questions_here * per_question
    cap = max(2, 2 * slot_count // n)
    head_dim = width // HEADS
    scale = 1.0 / math.sqrt(head_dim)
    ids = retrieved.reshape(slot_count)
    info = jnp.zeros((8, 128), jnp.int32).at[0, :slot_count].set(ids)
    info = info.at[1, :passages_here].set(valid_len)
    table, infos = gather_all(encoded.reshape(passages_here * passage_len, width), info, n)

    owner = ids // passages_here
    order = jnp.arange(slot_count, dtype=jnp.int32)
    before = order[None, :] < order[:, None]
    rank = jnp.sum((owner[:, None] == owner[None, :]) & before, axis=1).astype(jnp.int32)
    position = owner * cap + rank
    all_ids = infos[:, 0, :slot_count]
    lens = infos[:, 1, :passages_here].reshape(n * passages_here)

    slot_rows = table.reshape(n * passages_here, passage_len, width)[ids].reshape(
        slot_count * passage_len, width
    )
    slot_len = lens[ids]
    token_pos = jnp.arange(passage_len, dtype=jnp.int32)
    key_live = (token_pos[None, :] < slot_len[:, None]).reshape(
        questions_here, per_question * passage_len
    )
    dec_flat = decoder_states.reshape(questions_here * dec_len, width)
    cot_flat = cotangent.reshape(questions_here * dec_len, width)
    head_shape = (questions_here, dec_len, HEADS, head_dim)
    kv_shape = (questions_here, per_question * passage_len, HEADS, head_dim)
    dot = functools.partial(jnp.dot, preferred_element_type=F32)
    queries = dot(dec_flat, w_query).astype(BF).reshape(head_shape)
    context_grad = dot(cot_flat, w_output.T).astype(BF).reshape(head_shape)
    keys = dot(slot_rows, w_key).astype(BF)
    values = dot(slot_rows, w_value).astype(BF)
    context, query_grad, key_grad, value_grad = attend_core(
        queries, keys.reshape(kv_shape), values.reshape(kv_shape), key_live, context_grad, scale
    )
    ctx = context.reshape(questions_here * dec_len, width)
    qg = query_grad.reshape(questions_here * dec_len, width)
    kg = key_grad.reshape(slot_count * passage_len, width)
    vg = value_grad.reshape(slot_count * passage_len, width)
    attended = dot(ctx, w_output).astype(BF)
    d_decoder = dot(qg, w_query.T).astype(BF)
    share = (dot(kg, w_key.T) + dot(vg, w_value.T)).astype(BF)
    slots = (
        jnp.zeros((n * cap, passage_len, width), BF)
        .at[position]
        .set(share.reshape(slot_count, passage_len, width))
        .reshape(n, cap * passage_len, width)
    )
    parts = [dot(dec_flat.T, qg), dot(slot_rows.T, kg), dot(slot_rows.T, vg), dot(ctx.T, cot_flat)]
    rows = width // n
    grads = jnp.stack([part.astype(BF) for part in parts])
    grads = grads.reshape(4, n // 4, 2, 2, rows, width).transpose(3, 2, 1, 0, 4, 5)
    grads = grads.reshape(2, 2, n // 4, 4 * rows, width)
    got, summed = return_all(slots, grads, n)

    ask_owner = all_ids // passages_here
    before_b = before.astype(F32)
    mine = (ask_owner == me).astype(F32)
    ranks = jnp.einsum("si,ji->sj", mine, before_b)
    wanted_hot = (
        (all_ids[:, :, None] == me * passages_here + jnp.arange(passages_here))[:, :, None, :]
        & (ranks[:, :, None, None] == jnp.arange(cap, dtype=F32)[None, None, :, None])
    )
    select = jnp.any(wanted_hot, axis=1).astype(BF).reshape(n * cap, passages_here)
    d_encoded = lax.dot_general(
        select,
        got.reshape(n * cap, passage_len * width),
        (((0,), (0,)), ((), ())),
        preferred_element_type=F32,
    ).astype(BF)
    return (
        attended.reshape(decoder_states.shape),
        d_decoder.reshape(decoder_states.shape),
        d_encoded.reshape(encoded.shape),
        summed[0 * rows : 1 * rows],
        summed[1 * rows : 2 * rows],
        summed[2 * rows : 3 * rows],
        summed[3 * rows : 4 * rows],
    )


def solution(mesh):
    both = ("groups", "enc")
    in_specs = (
        P(both, None, None),
        P(both, None, None),
        P(both, None, None),
        P(both),
        P(both, None),
        P(),
        P(),
        P(),
        P(),
    )
    out_specs = (
        P(both, None, None),
        P(both, None, None),
        P(both, None, None),
        P(both, None),
        P(both, None),
        P(both, None),
        P(both, None),
    )
    return jax.shard_map(body, mesh=mesh, in_specs=in_specs, out_specs=out_specs, check_vma=False)
```

time: 643 us -> 338 us (0.53)
  waiting for transfers between devices: 366 us -> 0 us
  Pallas kernels: 0 us -> 181 us
  starting transfers between devices: 55.3 us -> 0 us
  local copies, waits for them, and re-layouts: 104 us -> 61.8 us
  between operations: 14.7 us -> 1.02 us
  blocking collectives: 13.6 us -> 0 us
    pallas_call x0 -> x2, Pallas kernels: none -> 181 us  [the longest x1 94.2 us: return_all(): pl.pallas_call(functools.partial(return_kernel, n), out_shape=(jax.ShapeD...]
    all_to_all x5 -> x0, waiting for transfers between devices: 156 us -> none  [the longest x1 55 us: body(): lax.all_to_all(value_table[chosen_rows].reshape(send_shape), 'enc', split...]
    unnamed x7 -> x0, waiting for transfers between devices: 143 us -> none
    reduce_scatter x1 -> x0, waiting for transfers between devices: 66.8 us -> none  [body(): lax.psum_scatter(grad_out_part, 'enc', scatter_dimension=0, tiled=True)]
    all_to_all x5 -> x0, starting transfers between devices: 54.9 us -> none  [the longest x1 15.8 us: body(): lax.all_to_all(key_table[chosen_rows].reshape(send_shape), 'enc', split_a...]
    all_to_all x1 -> x0, blocking collectives: 13.6 us -> none  [body(): lax.all_to_all(request.reshape(devices, capacity), 'enc', split_axis=0, c...]
    another operation x4 -> x3, local copies, waits for them, and re-layouts: 14.1 us -> 3.45 us  [the longest x1 2.61 us: body(): grads = jnp.stack([part.astype(BF) for part in parts])]
    gather x8 -> x2, local copies, waits for them, and re-layouts: 14 us -> 6.02 us  [the longest x1 5.22 us: body(): table.reshape(n * passages_here, passage_len, width)[ids]]
  transfers between devices with their start and end apart: 9 -> 0, of which waited for: 9 -> 0; matrix products, arithmetic and copies ran while one was open for 18% -> 0% of each run, Pallas kernels for 0% -> 0%
where the time goes in v1:
time: 338 us; the launch traced here: 334 us
  Pallas kernels  181 us (54%)
  matrix products  79.2 us (23%)
  local copies, waits for them, and re-layouts  61.8 us (18%)
  other arithmetic  10.4 us (3%)
    pallas_call x1, Pallas kernels, return_all(): pl.pallas_call(functools.partial(return_kernel, n), out_shape=(jax.ShapeD...  94.2 us
    pallas_call x1, Pallas kernels, gather_all(): pl.pallas_call(functools.partial(gather_kernel, n, cut), out_shape=(jax.S...  87.1 us
    dot_general x1, matrix products, attend_core(): jnp.einsum('qhts,qshd->qthd', score_grad, key_rows, preferred_element_typ...  21.6 us
    dot_general x1, matrix products, attend_core(): jnp.einsum('qhts,qthd->qshd', score_grad, queries, preferred_element_type...  21.5 us
    scatter x1, local copies, waits for them, and re-layouts, body(): slots = jnp.zeros((n * cap, passage_len, width), BF).at[position].set(sha...  9.46 us
    unnamed x53, local copies, waits for them, and re-layouts  7.96 us

profile of v1, /device:TPU:0, one launch (start us, length us, event | category | flops | bytes accessed | tf_op | source)
XLA Modules:
  0.0 333.7 jit_solution(7365296792897623015)
XLA Ops:
  4.6 87.1 %gather_passages.1 = (bf16[16,512,768]{2,1,0:T(8,128)(2,1)}, s32[16,8,128]{2,1,0:T(8,128)}) custom-call(bf16[512,768]{1,0:T(8,128)(2,1)} %bitcast.110, s32[8,128]{1,0:T(8,128)} %copy-done.20), custom_call_target="tpu_custom_call" | custom-call | tf_op jit(solution)/shard_map/gather_passages/pallas_call | solution.py:163
  91.7 5.2 %gather_fusion = bf16[64,16,768]{2,1,0:T(8,128)(2,1)S(1)} fusion(bf16[512,16,768]{2,1,0:T(8,128)(2,1)} %bitcast.113, s32[1024]{0:T(1024)S(1)} %pad_clamp_fusion), kind=kCustom, calls=%fused_computation | custom fusion | bytes 3145984 | tf_op jit(solution)/shard_map/gather | solution.py:324
  98.1 2.5 convolution_convert_fusion.2
  102.4 2.4 reshape.344
  110.0 2.3 fusion.31
  114.4 6.1 %fusion.72 = (f32[4,12,64]{2,1,0:T(8,128)}, f32[4,12,64,256]{3,2,1,0:T(8,128)}) fusion(f32[4,12,64,256]{3,2,1,0:T(8,128)} %fusion.31, pred[4,256]{1,0:T(4,128)(4,1)S(1)} %broadcast_compare_fusion.1), kind=kOutput, calls=%fused_computation.100 | output fusion | flops 4718847 | bytes 6304768 | tf_op jit(solution)/shard_map/sub | solution.py:286
  120.5 2.5 convolution_convert_fusion.3
  124.7 2.4 reshape.341
  127.1 2.6 convolution_convert_fusion.10
  129.8 2.5 reshape.391
  132.3 2.5 copy.62
  134.8 3.4 %fusion.27 = f32[4,12,64,256]{3,2,1,0:T(8,128)} fusion(bf16[4,64,12,64]{1,3,2,0:T(8,128)(2,1)} %copy.62, bf16[4,256,12,64]{1,0,3,2:T(4,128)(2,1)S(1)} %copy-done.4), kind=kOutput, calls=%fused_computation.35 | convolution fusion | flops 100663296 | bytes 5111808 | tf_op jit(solution)/shard_map/qthd,qshd->qhts/dot_general | solution.py:290
  138.2 21.5 %fusion.20 = bf16[4,256,12,64]{1,3,2,0:T(8,128)(2,1)S(1)} fusion(bf16[4,64,12,64]{1,3,2,0:T(8,128)(2,1)S(1)} %copy.60, f32[4,12,64,256]{3,2,1,0:T(8,128)} %fusion.27, f32[4,12,64,256]{3,2,1,0:T(8,128)} %get-tuple-element.46, f32[4,12,64]{2,1,0:T(8,128)} %get-tuple-element.45), kind=kOutput, calls=%fused_computation.31 | convolution fusion | flops 106958080 | bytes 8269824 | tf_op jit(solution)/shard_map/qhts,qthd->qshd/dot_general | solution.py:295
  162.6 2.5 convolution_convert_fusion.6
  165.1 21.6 %fusion.36 = bf16[4,64,12,64]{1,3,2,0:T(8,128)(2,1)S(1)} fusion(f32[4,12,64,256]{3,2,1,0:T(8,128)} %fusion.27, bf16[4,256,12,64]{1,0,3,2:T(4,128)(2,1)S(1)} %copy-done.3, f32[4,12,64,256]{3,2,1,0:T(8,128)} %get-tuple-element.46, f32[4,12,64]{2,1,0:T(8,128)} %get-tuple-element.45), kind=kOutput, calls=%fused_computation.42 | convolution fusion | flops 106368256 | bytes 8269824 | tf_op jit(solution)/shard_map/qhts,qshd->qthd/dot_general | solution.py:294
  189.3 2.5 fusion.23
  194.8 2.5 convolution_convert_fusion.5
  203.4 2.6 copy.68
  207.8 2.7 add_convert_fusion
  212.4 9.5 %scatter_fusion = bf16[128,16,768]{2,1,0:T(8,128)(2,1)} fusion(bf16[128,16,768]{2,1,0:T(8,128)(2,1)} %broadcast_in_dim.12, s32[64]{0:T(128)S(1)} %get-tuple-element.43, bf16[64,16,768]{2,1,0:T(8,128)(2,1)} %bitcast.95), kind=kCustom, calls=%fused_computation.2 | custom fusion | bytes 4718848 | tf_op jit(solution)/shard_map/scatter | solution.py:354
  221.8 94.2 %return_gradients.1 = (bf16[16,128,768]{2,1,0:T(8,128)(2,1)S(1)}, f32[192,768]{1,0:T(8,128)S(1)}) custom-call(bf16[16,128,768]{2,1,0:T(8,128)(2,1)} %bitcast.88, bf16[2,2,4,192,768]{4,3,2,1,0:T(8,128)(2,1)} %bitcast.89), custom_call_target="tpu_custom_call" | custom-call | tf_op jit(solution)/shard_map/return_gradients/pallas_call | solution.py:251
  317.7 5.7 %reshape.358 = bf16[128,12288]{1,0:T(8,128)(2,1)} reshape(bf16[16,128,768]{2,1,0:T(8,128)(2,1)} %copy-done.1) | data formatting | bytes 6291456 | tf_op jit(solution)/shard_map/reshape | solution.py:375
  324.6 2.3 and_reduce_fusion
  326.8 2.5 convolution_convert_fusion
  (96 shorter events, 40.9 us)
Async XLA Ops:
  0.6 97.5 %copy-start = (bf16[768,768]{1,0:T(8,128)(2,1)S(1)}, bf16[768,768]{1,0:T(8,128)(2,1)}, u32[]{:S(2)}) copy-start(bf16[768,768]{1,0:T(8,128)(2,1)} %param.19) | copy-start | bytes 3538948
  97.0 1.1 copy-start.12
  102.4 2.5 copy-start.17
  106.6 3.4 %copy-start.2 = (bf16[4,256,12,64]{1,0,3,2:T(4,128)(2,1)S(1)}, bf16[4,256,12,64]{1,0,3,2:T(4,128)(2,1)}, u32[]{:S(2)}) copy-start(bf16[4,256,12,64]{1,0,3,2:T(4,128)(2,1)} %reshape.344) | copy-start | bytes 4718596
  114.4 6.1 %copy-start.13 = (bf16[64,16,768]{2,1,0:T(8,128)(2,1)S(1)}, bf16[64,16,768]{2,1,0:T(8,128)(2,1)}, u32[]{:S(2)}) copy-start(bf16[64,16,768]{2,1,0:T(8,128)(2,1)} %copy-done.12) | copy-start | bytes 4718596
  114.4 6.1 %copy-start.21 = (bf16[768,768]{1,0:T(8,128)(2,1)S(1)}, bf16[768,768]{1,0:T(8,128)(2,1)}, u32[]{:S(2)}) copy-start(bf16[768,768]{1,0:T(8,128)(2,1)} %param.20) | copy-start | bytes 3538948
  129.8 5.0 %copy-start.4 = (bf16[4,256,12,64]{1,0,3,2:T(4,128)(2,1)S(1)}, bf16[4,256,12,64]{1,0,3,2:T(4,128)(2,1)}, u32[]{:S(2)}) copy-start(bf16[4,256,12,64]{1,0,3,2:T(4,128)(2,1)} %reshape.341) | copy-start | bytes 4718596
  160.9 1.6 copy-start.14
  161.3 3.8 %copy-start.8 = (bf16[96,8,4,256]{3,1,2,0:T(8,128)(2,1)}, bf16[96,8,4,256]{3,1,2,0:T(8,128)(2,1)S(1)}, u32[]{:S(2)}) copy-start(bf16[96,8,4,256]{3,1,2,0:T(8,128)(2,1)S(1)} %copy.73) | copy-start | bytes 4718596
  162.6 2.5 copy-start.3
  187.3 2.0 copy-start.7
  187.8 1.5 copy-start.24
  193.1 1.6 copy-start.15
  193.5 3.7 %copy-start.10 = (bf16[96,8,4,256]{3,1,2,0:T(8,128)(2,1)}, bf16[96,8,4,256]{3,1,2,0:T(8,128)(2,1)S(1)}, u32[]{:S(2)}) copy-start(bf16[96,8,4,256]{3,1,2,0:T(8,128)(2,1)S(1)} %copy.74) | copy-start | bytes 4718596
  194.8 2.5 copy-start.5
  194.8 2.5 copy-start.23
  200.0 1.7 copy-start.18
  203.4 2.6 copy-start.9
  206.0 1.5 copy-start.11
  206.1 1.7 copy-start.22
  316.1 1.7 copy-start.1
  329.3 1.9 copy-start.6
  330.4 2.1 copy-start.16
  330.4 2.1 copy-start.19
  (1 other events, 0.6 us)

commit v2 on v1

--- a/solution.py
+++ b/solution.py
@@ -245,23 +245,23 @@
 
 def return_all(slots, grads, n):
     depth = n // 4
-    high, width = grads.shape[-2:]
+    block = grads.shape[-3:]
     hbm = pl.BlockSpec(memory_space=pl.ANY)
     vmem = pl.BlockSpec(memory_space=pltpu.VMEM)
     return pl.pallas_call(
         functools.partial(return_kernel, n),
         out_shape=(
             jax.ShapeDtypeStruct(slots.shape, BF),
-            jax.ShapeDtypeStruct((high, width), F32),
+            jax.ShapeDtypeStruct(block, F32),
         ),
         in_specs=[hbm, vmem],
         out_specs=(hbm, vmem),
         scratch_shapes=[
-            pltpu.VMEM((2, depth, high, width), BF),
-            pltpu.VMEM((2, depth, high, width), BF),
-            pltpu.VMEM((depth, high, width), BF),
-            pltpu.VMEM((depth, high, width), BF),
-            pltpu.VMEM((depth, high, width), BF),
+            pltpu.VMEM((2, depth) + block, BF),
+            pltpu.VMEM((2, depth) + block, BF),
+            pltpu.VMEM((depth,) + block, BF),
+            pltpu.VMEM((depth,) + block, BF),
+            pltpu.VMEM((depth,) + block, BF),
             pltpu.SemaphoreType.DMA((2,)),
             pltpu.SemaphoreType.DMA((2,)),
             pltpu.SemaphoreType.DMA((depth,)),
@@ -277,23 +277,174 @@
     )(slots, grads)
 
 
-def attend_core(queries, key_rows, value_rows, key_live, context_grad, score_scale):
-    scores = (
-        jnp.einsum("qthd,qshd->qhts", queries, key_rows, preferred_element_type=F32) * score_scale
-    )
-    scores = jnp.where(key_live[:, None, None, :], scores, -1e30)
-    top = jnp.max(scores, axis=-1, keepdims=True)
-    expo = jnp.exp(scores - top)
-    probs = expo / jnp.sum(expo, axis=-1, keepdims=True)
-    probs_b = probs.astype(BF)
-    context = jnp.einsum("qhts,qshd->qthd", probs_b, value_rows, preferred_element_type=F32).astype(BF)
-    prob_grad = jnp.einsum("qthd,qshd->qhts", context_grad, value_rows, preferred_element_type=F32)
-    value_grad = jnp.einsum("qhts,qthd->qshd", probs_b, context_grad, preferred_element_type=F32).astype(BF)
-    inner = jnp.sum(probs * prob_grad, axis=-1, keepdims=True)
-    score_grad = (probs * (prob_grad - inner) * score_scale).astype(BF)
-    query_grad = jnp.einsum("qhts,qshd->qthd", score_grad, key_rows, preferred_element_type=F32).astype(BF)
-    key_grad = jnp.einsum("qhts,qthd->qshd", score_grad, queries, preferred_element_type=F32).astype(BF)
-    return (context, query_grad, key_grad, value_grad)
+def attend_kernel(
+    n, cap, per_owner, dims, ids_ref, infos_ref, dec_ref, cot_ref, table_ref, wq_ref, wk_ref, wv_ref, wo_ref,
+    att_ref, ddec_ref, slots_ref, g_ref,
+    rows, rows_t, keys, values, kg, vg, queries, cgrad, ctx, qg, flip, bias, counts, where_to, sems,
+):
+    questions, tokens, slots_per, length = dims
+    slot_count = questions * slots_per
+    span = slots_per * length
+    width = dec_ref.shape[1]
+    scale = 1.0 / math.sqrt(width // HEADS)
+    high = width // n
+    tile = 256
+
+    def nn(a, b):
+        return lax.dot_general(a, b, (((1,), (0,)), ((), ())), preferred_element_type=F32)
+
+    def nt(a, b):
+        return lax.dot_general(a, b, (((1,), (1,)), ((), ())), preferred_element_type=F32)
+
+    def tn(a, b):
+        return lax.dot_general(a, b, (((0,), (0,)), ((), ())), preferred_element_type=F32)
+
+    def fetch(j):
+        return pltpu.make_async_copy(
+            table_ref.at[ids_ref[j]], rows.at[pl.ds(j * length, length)], sems.at[j]
+        )
+
+    def clear(i, carry):
+        counts[i] = 0
+        return carry
+
+    lax.fori_loop(0, n, clear, 0)
+    token_at = lax.broadcasted_iota(jnp.int32, (length, 128), 0)
+
+    def begin(j, carry):
+        fetch(j).start()
+        passage = ids_ref[j]
+        owner = passage // per_owner
+        where_to[j] = owner * cap + counts[owner]
+        counts[owner] = counts[owner] + 1
+        live = infos_ref[owner, 1, passage - owner * per_owner]
+        bias[pl.ds(pl.multiple_of(j * length, length), length), :] = jnp.where(token_at < live, 0.0, -1e30)
+        return carry
+
+    lax.fori_loop(0, slot_count, begin, 0)
+
+    def wipe(i, carry):
+        slots_ref[i] = jnp.zeros((length, width), BF)
+        return carry
+
+    lax.fori_loop(0, n * cap, wipe, 0)
+    queries[...] = nn(dec_ref[...], wq_ref[...]).astype(BF)
+    cgrad[...] = nt(cot_ref[...], wo_ref[...]).astype(BF)
+
+    def finish(j, carry):
+        fetch(j).wait()
+        return carry
+
+    lax.fori_loop(0, slot_count, finish, 0)
+
+    def project(i, carry):
+        at = pl.ds(pl.multiple_of(i * span, span), span)
+        block = rows[at, :]
+        keys[at, :] = nn(block, wk_ref[...]).astype(BF)
+        values[at, :] = nn(block, wv_ref[...]).astype(BF)
+        rows_t[:, at] = block.T
+        return carry
+
+    lax.fori_loop(0, questions, project, 0)
+    low = lax.broadcasted_iota(jnp.int32, (tokens, 128), 1) < 64
+
+    def attend(q, carry):
+        kat = pl.ds(pl.multiple_of(q * span, span), span)
+        tat = pl.ds(pl.multiple_of(q * tokens, tokens), tokens)
+        dead = bias[kat, :]
+        for pair in range(width // 128):
+            cols = pl.ds(pair * 128, 128)
+            qp, cp = queries[tat, cols], cgrad[tat, cols]
+            zero = jnp.zeros_like(qp)
+            q2 = jnp.concatenate([jnp.where(low, qp, zero), jnp.where(low, zero, qp)], axis=0)
+            c2 = jnp.concatenate([jnp.where(low, cp, zero), jnp.where(low, zero, cp)], axis=0)
+            kp, vp = keys[kat, cols], values[kat, cols]
+            scores = nt(kp, q2) * scale + dead
+            top = jnp.max(scores, axis=0, keepdims=True)
+            expo = jnp.exp(scores - top)
+            probs = expo / jnp.sum(expo, axis=0, keepdims=True)
+            probs_b = probs.astype(BF)
+            both = tn(probs_b, vp)
+            ctx[tat, cols] = jnp.where(low, both[:tokens], both[tokens:]).astype(BF)
+            vg[kat, cols] = nn(probs_b, c2).astype(BF)
+            pgrad = nt(vp, c2)
+            inner = jnp.sum(probs * pgrad, axis=0, keepdims=True)
+            sgrad = (probs * (pgrad - inner) * scale).astype(BF)
+            both_q = tn(sgrad, kp)
+            qg[tat, cols] = jnp.where(low, both_q[:tokens], both_q[tokens:]).astype(BF)
+            kg[kat, cols] = nn(sgrad, q2).astype(BF)
+        return carry
+
+    lax.fori_loop(0, questions, attend, 0)
+    att_ref[...] = nn(ctx[...], wo_ref[...]).astype(BF)
+    ddec_ref[...] = nt(qg[...], wq_ref[...]).astype(BF)
+
+    def back(i, carry):
+        at = pl.ds(pl.multiple_of(i * span, span), span)
+        share = (nt(kg[at, :], wk_ref[...]) + nt(vg[at, :], wv_ref[...])).astype(BF)
+        for j in range(slots_per):
+            slots_ref[where_to[i * slots_per + j]] = share[j * length : (j + 1) * length]
+        return carry
+
+    lax.fori_loop(0, questions, back, 0)
+
+    def spread(which, left, right):
+        def one(i, carry):
+            cols = pl.ds(pl.multiple_of(i * tile, tile), tile)
+            part = nn(left[...], right[:, cols])
+            for e in range(n):
+                z, y, c = place(e)
+                g_ref[c, y, z, which, :, cols] = part[e * high : (e + 1) * high].astype(BF)
+            return carry
+
+        lax.fori_loop(0, width // tile, one, 0)
+
+    spread(1, rows_t, kg)
+    spread(2, rows_t, vg)
+    flip[...] = dec_ref[...].T
+    spread(0, flip, qg)
+    flip[...] = ctx[...].T
+    spread(3, flip, cot_ref)
+
+
+def attend_all(ids, infos, dec, cot, table, weights, n, cap, dims):
+    questions, tokens, slots_per, length = dims
+    width = dec.shape[1]
+    slot_rows = questions * slots_per * length
+    smem = pl.BlockSpec(memory_space=pltpu.SMEM)
+    vmem = pl.BlockSpec(memory_space=pltpu.VMEM)
+    hbm = pl.BlockSpec(memory_space=pl.ANY)
+    shape = jax.ShapeDtypeStruct
+    return pl.pallas_call(
+        functools.partial(attend_kernel, n, cap, table.shape[0] // n, dims),
+        out_shape=(
+            shape(dec.shape, BF),
+            shape(dec.shape, BF),
+            shape((n * cap, length, width), BF),
+            shape((2, 2, n // 4, 4, width // n, width), BF),
+        ),
+        in_specs=[smem, smem, vmem, vmem, hbm, vmem, vmem, vmem, vmem],
+        out_specs=(vmem,) * 4,
+        scratch_shapes=[
+            pltpu.VMEM((slot_rows, width), BF),
+            pltpu.VMEM((width, slot_rows), BF),
+            pltpu.VMEM((slot_rows, width), BF),
+            pltpu.VMEM((slot_rows, width), BF),
+            pltpu.VMEM((slot_rows, width), BF),
+            pltpu.VMEM((slot_rows, width), BF),
+            pltpu.VMEM(dec.shape, BF),
+            pltpu.VMEM(dec.shape, BF),
+            pltpu.VMEM(dec.shape, BF),
+            pltpu.VMEM(dec.shape, BF),
+            pltpu.VMEM((width, dec.shape[0]), BF),
+            pltpu.VMEM((slot_rows, 128), F32),
+            pltpu.SMEM((n,), jnp.int32),
+            pltpu.SMEM((questions * slots_per,), jnp.int32),
+            pltpu.SemaphoreType.DMA((questions * slots_per,)),
+        ],
+        compiler_params=pltpu.CompilerParams(vmem_limit_bytes=56 * 2**20),
+        name="attend",
+    )(ids, infos, dec, cot, table, *weights)
 
 
 def body(
@@ -306,84 +457,49 @@
     per_question = retrieved.shape[1]
     slot_count = questions_here * per_question
     cap = max(2, 2 * slot_count // n)
-    head_dim = width // HEADS
-    scale = 1.0 / math.sqrt(head_dim)
     ids = retrieved.reshape(slot_count)
     info = jnp.zeros((8, 128), jnp.int32).at[0, :slot_count].set(ids)
     info = info.at[1, :passages_here].set(valid_len)
     table, infos = gather_all(encoded.reshape(passages_here * passage_len, width), info, n)
 
-    owner = ids // passages_here
+    all_ids = infos[:, 0, :slot_count]
+    attended, d_decoder, slots, grads = attend_all(
+        ids,
+        infos,
+        decoder_states.reshape(questions_here * dec_len, width),
+        cotangent.reshape(questions_here * dec_len, width),
+        table.reshape(n * passages_here, passage_len, width),
+        (w_query, w_key, w_value, w_output),
+        n,
+        cap,
+        (questions_here, dec_len, per_question, passage_len),
+    )
+    got, summed = return_all(slots.reshape(n, cap * passage_len, width), grads, n)
+
+    ask_owner = all_ids // passages_here
     order = jnp.arange(slot_count, dtype=jnp.int32)
-    before = order[None, :] < order[:, None]
-    rank = jnp.sum((owner[:, None] == owner[None, :]) & before, axis=1).astype(jnp.int32)
-    position = owner * cap + rank
-    all_ids = infos[:, 0, :slot_count]
-    lens = infos[:, 1, :passages_here].reshape(n * passages_here)
-
-    slot_rows = table.reshape(n * passages_here, passage_len, width)[ids].reshape(
-        slot_count * passage_len, width
-    )
-    slot_len = lens[ids]
+    before = (order[:, None] < order[None, :]).astype(F32)
+    mine = ask_owner == me
+    ranks = jnp.dot(mine.astype(F32), before)
+    hit = mine[:, None, :] & (ranks[:, None, :] == jnp.arange(cap, dtype=F32)[None, :, None])
+    local = all_ids - me * passages_here + 1
+    wanted = jnp.sum(jnp.where(hit, local[:, None, :], 0), axis=2) - 1
     token_pos = jnp.arange(passage_len, dtype=jnp.int32)
-    key_live = (token_pos[None, :] < slot_len[:, None]).reshape(
-        questions_here, per_question * passage_len
-    )
-    dec_flat = decoder_states.reshape(questions_here * dec_len, width)
-    cot_flat = cotangent.reshape(questions_here * dec_len, width)
-    head_shape = (questions_here, dec_len, HEADS, head_dim)
-    kv_shape = (questions_here, per_question * passage_len, HEADS, head_dim)
-    dot = functools.partial(jnp.dot, preferred_element_type=F32)
-    queries = dot(dec_flat, w_query).astype(BF).reshape(head_shape)
-    context_grad = dot(cot_flat, w_output.T).astype(BF).reshape(head_shape)
-    keys = dot(slot_rows, w_key).astype(BF)
-    values = dot(slot_rows, w_value).astype(BF)
-    context, query_grad, key_grad, value_grad = attend_core(
-        queries, keys.reshape(kv_shape), values.reshape(kv_shape), key_live, context_grad, scale
-    )
-    ctx = context.reshape(questions_here * dec_len, width)
-    qg = query_grad.reshape(questions_here * dec_len, width)
-    kg = key_grad.reshape(slot_count * passage_len, width)
-    vg = value_grad.reshape(slot_count * passage_len, width)
-    attended = dot(ctx, w_output).astype(BF)
-    d_decoder = dot(qg, w_query.T).astype(BF)
-    share = (dot(kg, w_key.T) + dot(vg, w_value.T)).astype(BF)
-    slots = (
-        jnp.zeros((n * cap, passage_len, width), BF)
-        .at[position]
-        .set(share.reshape(slot_count, passage_len, width))
-        .reshape(n, cap * passage_len, width)
-    )
-    parts = [dot(dec_flat.T, qg), dot(slot_rows.T, kg), dot(slot_rows.T, vg), dot(ctx.T, cot_flat)]
-    rows = width // n
-    grads = jnp.stack([part.astype(BF) for part in parts])
-    grads = grads.reshape(4, n // 4, 2, 2, rows, width).transpose(3, 2, 1, 0, 4, 5)
-    grads = grads.reshape(2, 2, n // 4, 4 * rows, width)
-    got, summed = return_all(slots, grads, n)
-
-    ask_owner = all_ids // passages_here
-    before_b = before.astype(F32)
-    mine = (ask_owner == me).astype(F32)
-    ranks = jnp.einsum("si,ji->sj", mine, before_b)
-    wanted_hot = (
-        (all_ids[:, :, None] == me * passages_here + jnp.arange(passages_here))[:, :, None, :]
-        & (ranks[:, :, None, None] == jnp.arange(cap, dtype=F32)[None, None, :, None])
-    )
-    select = jnp.any(wanted_hot, axis=1).astype(BF).reshape(n * cap, passages_here)
-    d_encoded = lax.dot_general(
-        select,
-        got.reshape(n * cap, passage_len * width),
-        (((0,), (0,)), ((), ())),
-        preferred_element_type=F32,
+    sent_row = (wanted[:, :, None] * passage_len + token_pos).reshape(n * cap * passage_len)
+    sent_row = jnp.where(sent_row < 0, -1, sent_row)
+    own_row = jnp.arange(passages_here * passage_len, dtype=jnp.int32)
+    select = (own_row[:, None] == sent_row[None, :]).astype(BF)
+    d_encoded = jnp.dot(
+        select, got.reshape(n * cap * passage_len, width), preferred_element_type=F32
     ).astype(BF)
     return (
         attended.reshape(decoder_states.shape),
         d_decoder.reshape(decoder_states.shape),
         d_encoded.reshape(encoded.shape),
-        summed[0 * rows : 1 * rows],
-        summed[1 * rows : 2 * rows],
-        summed[2 * rows : 3 * rows],
-        summed[3 * rows : 4 * rows],
+        summed[0],
+        summed[1],
+        summed[2],
+        summed[3],
     )
 
 

time: 338 us -> 234 us (0.69)
  matrix products: 79.2 us -> 4.83 us
  local copies, waits for them, and re-layouts: 61.8 us -> 5.94 us
  Pallas kernels: 181 us -> 217 us
  other arithmetic: 10.4 us -> 2.18 us
    dot_general x20 -> x2, matrix products: 79.2 us -> 4.83 us  [the longest x1 4.7 us: body(): jnp.dot(select, got.reshape(n * cap * passage_len, width), preferred_elem...]
    pallas_call x0 -> x1, Pallas kernels: none -> 35.4 us  [attend_all(): pl.pallas_call(functools.partial(attend_kernel, n, cap, table.shape[0] //...]
    reshape x9 -> x0, local copies, waits for them, and re-layouts: 20.6 us -> none  [the longest x1 5.71 us: body(): got.reshape(n * cap, passage_len * width)]
    scatter x1 -> x0, local copies, waits for them, and re-layouts: 9.46 us -> none  [body(): slots = jnp.zeros((n * cap, passage_len, width), BF).at[position].set(sha...]
    convert_element_type x6 -> x0, local copies, waits for them, and re-layouts: 7.11 us -> none  [the longest x1 1.71 us: body(): keys = dot(slot_rows, w_key).astype(BF)]
    sub x1 -> x0, other arithmetic: 6.07 us -> none  [attend_core(): expo = jnp.exp(scores - top)]
    gather x2 -> x0, local copies, waits for them, and re-layouts: 6.02 us -> none  [the longest x1 5.22 us: body(): table.reshape(n * passages_here, passage_len, width)[ids]]
    unnamed x53 -> x5, local copies, waits for them, and re-layouts: 7.96 us -> 2.23 us
where the time goes in v2:
time: 234 us; the launch traced here: 230 us
  Pallas kernels  217 us (93%)
  local copies, waits for them, and re-layouts  5.94 us (3%)
  matrix products  4.83 us (2%)
    pallas_call x1, Pallas kernels, return_all(): pl.pallas_call(functools.partial(return_kernel, n), out_shape=(jax.ShapeD...  94.3 us
    pallas_call x1, Pallas kernels, gather_all(): pl.pallas_call(functools.partial(gather_kernel, n, cut), out_shape=(jax.S...  87.1 us
    pallas_call x1, Pallas kernels, attend_all(): pl.pallas_call(functools.partial(attend_kernel, n, cap, table.shape[0] //...  35.4 us
    dot_general x1, matrix products, body(): jnp.dot(select, got.reshape(n * cap * passage_len, width), preferred_elem...  4.7 us

profile of v2, /device:TPU:0, one launch (start us, length us, event | category | flops | bytes accessed | tf_op | source)
XLA Modules:
  0.0 230.4 jit_solution(15771106947116542603)
XLA Ops:
  0.6 1.3 reshape.126.ids_ref
  1.9 0.8 reshape.128
  2.7 0.8 scatter.9.info_ref
  3.4 0.0 copy-start.1
  3.5 0.6 copy-done.1
  4.0 87.1 %gather_passages.1 = (bf16[16,512,768]{2,1,0:T(8,128)(2,1)}, s32[16,8,128]{2,1,0:T(8,128)}) custom-call(bf16[512,768]{1,0:T(8,128)(2,1)} %bitcast.27, s32[8,128]{1,0:T(8,128)} %copy-done.1), custom_call_target="tpu_custom_call" | custom-call | tf_op jit(solution)/shard_map/gather_passages/pallas_call | solution.py:163
  91.2 35.4 %attend.1 = (bf16[256,768]{1,0:T(8,128)(2,1)}, bf16[256,768]{1,0:T(8,128)(2,1)}, bf16[128,16,768]{2,1,0:T(8,128)(2,1)}, bf16[2,2,4,4,48,768]{5,4,3,2,1,0:T(8,128)(2,1)}) custom-call(s32[64]{0:T(128)} %reshape.126.ids_ref, s32[16,8,128]{2,1,0:T(8,128)} %get-tuple-element.39.infos_ref, bf16[256,768]{1,0:T(8,128)(2,1)} %bitcast.28, bf16[256,768]{1,0:T(8,128)(2,1)} %bitcast.29, ...), custom_call_target="tpu_custom_call" | custom-call | tf_op jit(solution)/shard_map/attend/pallas_call | solution.py:418
  126.6 94.3 %return_gradients.1 = (bf16[16,128,768]{2,1,0:T(8,128)(2,1)S(1)}, f32[4,48,768]{2,1,0:T(8,128)S(1)}) custom-call(bf16[16,128,768]{2,1,0:T(8,128)(2,1)} %bitcast.26, bf16[2,2,4,4,48,768]{5,4,3,2,1,0:T(8,128)(2,1)} %get-tuple-element.44.g_ref), custom_call_target="tpu_custom_call" | custom-call | tf_op jit(solution)/shard_map/return_gradients/pallas_call | solution.py:251
  220.8 0.0 copy-start
  220.8 1.6 copy-done
  222.5 0.8 fusion.23
  223.3 0.1 fusion.4
  223.5 0.9 fusion.7
  224.4 0.3 select_reduce_fusion
  224.7 0.1 iota_add_fusion
  224.8 0.1 add.43
  224.9 4.7 %fusion.2 = bf16[512,768]{1,0:T(8,128)(2,1)} fusion(bf16[2048,768]{1,0:T(8,128)(2,1)} %bitcast.24, s32[2048]{0:T(1024)S(1)} %compare_select_fusion), kind=kOutput, calls=%fused_computation.3 | convolution fusion | flops 1612054528 | bytes 3940352 | tf_op jit(solution)/shard_map/dot_general | solution.py:492
  229.6 0.8 slice_bitcast_fusion
  (4 shorter events, 0.0 us)
Async XLA Ops:
  3.4 0.6 copy-start.1
  220.8 1.6 copy-start

commit v3 on v2

--- a/solution.py
+++ b/solution.py
@@ -32,25 +32,29 @@
 
 
 def gather_kernel(
-    n, cut, enc_ref, info_ref, table_ref, infos_ref, send_sem, recv_sem, info_send, info_recv, own_sem
+    n, cuts, enc_ref, ids_ref, len_ref, table_ref, infos_ref,
+    info_ref, send_sem, recv_sem, info_send, info_recv, own_sem,
 ):
     depth = n // 4
     me = lax.axis_index("enc")
     z, y, c = place(me)
-    rows = enc_ref.shape[0]
-    spans = (pl.ds(0, cut), pl.ds(cut, rows - cut))
+    spans = [pl.ds(a, b - a) for a, b in zip(cuts[:-1], cuts[1:])]
+    last = len(spans) - 1
+    info_ref[...] = jnp.zeros_like(info_ref)
+    info_ref[0 : ids_ref.shape[0], 0 : ids_ref.shape[1]] = ids_ref[...]
+    info_ref[ids_ref.shape[0] : ids_ref.shape[0] + 1, 0 : len_ref.shape[1]] = len_ref[...]
     greet_all(n, me)
 
     owns = [pltpu.make_async_copy(enc_ref, table_ref.at[me], own_sem.at[0])]
     owns.append(pltpu.make_async_copy(info_ref, infos_ref.at[me], own_sem.at[1]))
     sends = []
 
-    def send(cond, src, origin, half, kind, target):
+    def send(cond, src, origin, part, kind, target):
         copy = pltpu.make_async_remote_copy(
             src_ref=src,
-            dst_ref=table_ref.at[origin, spans[half]],
-            send_sem=send_sem.at[kind, half, origin],
-            recv_sem=recv_sem.at[half, origin],
+            dst_ref=table_ref.at[origin, spans[part]],
+            send_sem=send_sem.at[kind, part, origin],
+            recv_sem=recv_sem.at[part, origin],
             device_id={"enc": target},
             device_id_type=MESH,
         )
@@ -60,12 +64,12 @@
         else:
             pl.when(cond)(copy.start)
 
-    def arrive(cond, origin, half):
+    def arrive(cond, origin, part):
         copy = pltpu.make_async_remote_copy(
-            src_ref=table_ref.at[origin, spans[half]],
-            dst_ref=table_ref.at[origin, spans[half]],
-            send_sem=send_sem.at[0, half, origin],
-            recv_sem=recv_sem.at[half, origin],
+            src_ref=table_ref.at[origin, spans[part]],
+            dst_ref=table_ref.at[origin, spans[part]],
+            send_sem=send_sem.at[0, part, origin],
+            recv_sem=recv_sem.at[part, origin],
             device_id={"enc": me},
             device_id_type=MESH,
         )
@@ -81,14 +85,11 @@
     sibling = index_of(z, y, 1 - c)
 
     own = [enc_ref.at[span] for span in spans]
-    send(None, own[1], me, 1, 2, across)
-    send(up_ok, own[0], me, 0, 0, up)
-    send(down_ok, own[0], me, 0, 1, down)
-    send(None, own[0], me, 0, 2, across)
-    send(up_ok, own[1], me, 1, 0, up)
-    send(down_ok, own[1], me, 1, 1, down)
-    for half in range(2):
-        send(None, own[half], me, half, 3, sibling)
+    for part in range(last):
+        send(up_ok, own[part], me, part, 0, up)
+        send(down_ok, own[part], me, part, 1, down)
+        send(None, own[part], me, part, 2, across)
+    send(None, own[last], me, last, 2, across)
     info_copies = []
     for k in range(1, n):
         copy = pltpu.make_async_remote_copy(
@@ -101,41 +102,60 @@
         )
         copy.start()
         info_copies.append(copy)
+    for part in range(last + 1):
+        send(None, own[part], me, part, 3, sibling)
     for copy in owns:
         copy.start()
 
-    def passed(cond, origin, half, go_up, go_down, go_across):
-        arrive(cond, origin, half)
-        block = table_ref.at[origin, spans[half]]
+    def passed(cond, origin, part, go_up, go_down, go_across):
+        arrive(cond, origin, part)
+        block = table_ref.at[origin, spans[part]]
         both = lambda a: a if cond is None else jnp.logical_and(cond, a)
         if go_up:
-            send(both(up_ok), block, origin, half, 0, up)
+            send(both(up_ok), block, origin, part, 0, up)
         if go_down:
-            send(both(down_ok), block, origin, half, 1, down)
+            send(both(down_ok), block, origin, part, 1, down)
         if go_across:
-            send(cond, block, origin, half, 2, across)
-        send(cond, block, origin, half, 3, sibling)
-
-    passed(None, across, 1, True, True, False)
+            send(cond, block, origin, part, 2, across)
+        send(cond, block, origin, part, 3, sibling)
+
+    def along(d, sign):
+        zo = z - sign * d
+        return jnp.logical_and(zo >= 0, zo < depth), jnp.clip(zo, 0, depth - 1)
+
+    def late(d):
+        if d == 0:
+            send(up_ok, own[last], me, last, 0, up)
+            send(down_ok, own[last], me, last, 1, down)
+            passed(None, across, last, True, True, False)
+            return
+        for sign in (1, -1):
+            cond, zc = along(d, sign)
+            for row in (y, 1 - y):
+                passed(cond, index_of(zc, row, c), last, sign > 0, sign < 0, False)
+
+    def crossed(d):
+        for part in range(last):
+            if d == 0:
+                passed(None, across, part, False, False, False)
+                continue
+            for sign in (1, -1):
+                cond, zc = along(d, sign)
+                passed(cond, index_of(zc, 1 - y, c), part, False, False, False)
+
     for d in range(1, depth):
-        for sign in (1, -1):
-            zo = z - sign * d
-            cond = jnp.logical_and(zo >= 0, zo < depth)
-            zc = jnp.clip(zo, 0, depth - 1)
-            passed(cond, index_of(zc, y, c), 0, sign > 0, sign < 0, True)
-            passed(cond, index_of(zc, y, c), 1, sign > 0, sign < 0, False)
-            passed(cond, index_of(zc, 1 - y, c), 1, sign > 0, sign < 0, False)
-        if d == 1:
-            passed(None, across, 0, False, False, False)
-        for sign in (1, -1):
-            zo = z - sign * d
-            cond = jnp.logical_and(zo >= 0, zo < depth)
-            zc = jnp.clip(zo, 0, depth - 1)
-            passed(cond, index_of(zc, 1 - y, c), 0, False, False, False)
+        for part in range(last):
+            for sign in (1, -1):
+                cond, zc = along(d, sign)
+                passed(cond, index_of(zc, y, c), part, sign > 0, sign < 0, True)
+        late(d - 1)
+        crossed(d - 1)
+    late(depth - 1)
+    crossed(depth - 1)
     for zo in range(depth):
         for yo in range(2):
-            for half in range(2):
-                arrive(None, index_of(zo, yo, 1 - c), half)
+            for part in range(last + 1):
+                arrive(None, index_of(zo, yo, 1 - c), part)
     for cond, copy in sends:
         if cond is None:
             copy.wait_send()
@@ -156,32 +176,36 @@
         copy.wait()
 
 
-def gather_all(encoded_flat, info, n):
+def gather_all(encoded_flat, retrieved, valid_len, n):
     rows, width = encoded_flat.shape
-    cut = rows * 13 // 16 // 16 * 16
+    cut = rows * 13 // 16 // 32 * 32
+    cuts = (0, cut // 2, cut, rows)
+    parts = len(cuts) - 1
     hbm = pl.BlockSpec(memory_space=pl.ANY)
+    vmem = pl.BlockSpec(memory_space=pltpu.VMEM)
     return pl.pallas_call(
-        functools.partial(gather_kernel, n, cut),
+        functools.partial(gather_kernel, n, cuts),
         out_shape=(
             jax.ShapeDtypeStruct((n, rows, width), BF),
-            jax.ShapeDtypeStruct((n,) + info.shape, jnp.int32),
+            jax.ShapeDtypeStruct((n, 8, 128), jnp.int32),
         ),
-        in_specs=[hbm, hbm],
+        in_specs=[hbm, vmem, vmem],
         out_specs=(hbm, hbm),
         scratch_shapes=[
-            pltpu.SemaphoreType.DMA((4, 2, n)),
-            pltpu.SemaphoreType.DMA((2, n)),
+            pltpu.VMEM((8, 128), jnp.int32),
+            pltpu.SemaphoreType.DMA((4, parts, n)),
+            pltpu.SemaphoreType.DMA((parts, n)),
             pltpu.SemaphoreType.DMA((n,)),
             pltpu.SemaphoreType.DMA((n,)),
             pltpu.SemaphoreType.DMA((2,)),
         ],
         compiler_params=pltpu.CompilerParams(collective_id=0, has_side_effects=True),
         name="gather_passages",
-    )(encoded_flat, info)
+    )(encoded_flat, retrieved, valid_len)
 
 
 def return_kernel(
-    n, slots_ref, g_ref, got_ref, gout_ref, r1, s1, r2, s2, r3, sem1, sem2, send3, recv3, send_a, recv_a, own_sem
+    n, slots_ref, g_ref, got_ref, gout_ref, r1, s1, r2, s2, s3, r3, sem1, sem2, send3, recv3, send_a, recv_a, own_sem
 ):
     depth = n // 4
     me = lax.axis_index("enc")
@@ -223,19 +247,45 @@
         return carry
 
     lax.fori_loop(0, depth, add2, 0)
-    thirds = []
-    for k in range(1, depth):
-        zt = lax.rem(z + k, depth)
-        copy = remote(s2.at[zt], r3.at[z], send3.at[k], recv3.at[z], index_of(zt, y, c))
-        copy.start()
-        thirds.append(copy)
-    for k in range(1, depth):
-        thirds[k - 1].wait_send()
-        zs = lax.rem(z + depth - k, depth)
-        remote(s2.at[zs], r3.at[zs], send3.at[k], recv3.at[zs], index_of(zs, y, c)).wait_recv()
+    for hop in range(depth - 1, 0, -1):
+        for way, sign in ((0, 1), (1, -1)):
+            t = z + sign * hop
+            inside = jnp.logical_and(t >= 0, t < depth)
+            has_back = jnp.logical_and(z - sign >= 0, z - sign < depth)
+            tc = jnp.clip(t, 0, depth - 1)
+            ahead = index_of(jnp.clip(z + sign, 0, depth - 1), y, c)
+            behind = jnp.logical_and(inside, has_back)
+
+            @pl.when(jnp.logical_and(inside, jnp.logical_not(has_back)))
+            def _(way=way, tc=tc):
+                s3[way, tc] = s2[tc]
+
+            @pl.when(behind)
+            def _(way=way, tc=tc):
+                remote(s3.at[way, tc], r3.at[way, tc], send3.at[way, tc], recv3.at[way, tc], me).wait_recv()
+                s3[way, tc] = (s2[tc].astype(F32) + r3[way, tc].astype(F32)).astype(BF)
+
+            @pl.when(inside)
+            def _(way=way, tc=tc, ahead=ahead):
+                remote(s3.at[way, tc], r3.at[way, tc], send3.at[way, tc], recv3.at[way, tc], ahead).start()
+
     gout_ref[...] = s2[z].astype(F32)
-    for k in range(1, depth):
-        gout_ref[...] += r3[lax.rem(z + k, depth)].astype(F32)
+    for way, sign in ((0, 1), (1, -1)):
+
+        @pl.when(jnp.logical_and(z - sign >= 0, z - sign < depth))
+        def _(way=way):
+            remote(s3.at[way, z], r3.at[way, z], send3.at[way, z], recv3.at[way, z], me).wait_recv()
+            gout_ref[...] += r3[way, z].astype(F32)
+
+    for hop in range(1, depth):
+        for way, sign in ((0, 1), (1, -1)):
+            t = z + sign * hop
+            tc = jnp.clip(t, 0, depth - 1)
+
+            @pl.when(jnp.logical_and(t >= 0, t < depth))
+            def _(way=way, tc=tc):
+                remote(s3.at[way, tc], r3.at[way, tc], send3.at[way, tc], recv3.at[way, tc], me).wait_send()
+
     for k in range(1, n):
         slot_copies[k - 1].wait_send()
         source = lax.rem(me + n - k, n)
@@ -261,11 +311,12 @@
             pltpu.VMEM((2, depth) + block, BF),
             pltpu.VMEM((depth,) + block, BF),
             pltpu.VMEM((depth,) + block, BF),
-            pltpu.VMEM((depth,) + block, BF),
+            pltpu.VMEM((2, depth) + block, BF),
+            pltpu.VMEM((2, depth) + block, BF),
             pltpu.SemaphoreType.DMA((2,)),
             pltpu.SemaphoreType.DMA((2,)),
-            pltpu.SemaphoreType.DMA((depth,)),
-            pltpu.SemaphoreType.DMA((depth,)),
+            pltpu.SemaphoreType.DMA((2, depth)),
+            pltpu.SemaphoreType.DMA((2, depth)),
             pltpu.SemaphoreType.DMA((n,)),
             pltpu.SemaphoreType.DMA((n,)),
             pltpu.SemaphoreType.DMA(()),
@@ -301,7 +352,7 @@
 
     def fetch(j):
         return pltpu.make_async_copy(
-            table_ref.at[ids_ref[j]], rows.at[pl.ds(j * length, length)], sems.at[j]
+            table_ref.at[ids_ref[j // slots_per, j % slots_per]], rows.at[pl.ds(j * length, length)], sems.at[j]
         )
 
     def clear(i, carry):
@@ -313,11 +364,11 @@
 
     def begin(j, carry):
         fetch(j).start()
-        passage = ids_ref[j]
+        passage = ids_ref[j // slots_per, j % slots_per]
         owner = passage // per_owner
         where_to[j] = owner * cap + counts[owner]
         counts[owner] = counts[owner] + 1
-        live = infos_ref[owner, 1, passage - owner * per_owner]
+        live = infos_ref[owner, questions, passage - owner * per_owner]
         bias[pl.ds(pl.multiple_of(j * length, length), length), :] = jnp.where(token_at < live, 0.0, -1e30)
         return carry
 
@@ -362,7 +413,7 @@
             scores = nt(kp, q2) * scale + dead
             top = jnp.max(scores, axis=0, keepdims=True)
             expo = jnp.exp(scores - top)
-            probs = expo / jnp.sum(expo, axis=0, keepdims=True)
+            probs = expo * (1.0 / jnp.sum(expo, axis=0, keepdims=True))
             probs_b = probs.astype(BF)
             both = tn(probs_b, vp)
             ctx[tat, cols] = jnp.where(low, both[:tokens], both[tokens:]).astype(BF)
@@ -457,14 +508,15 @@
     per_question = retrieved.shape[1]
     slot_count = questions_here * per_question
     cap = max(2, 2 * slot_count // n)
-    ids = retrieved.reshape(slot_count)
-    info = jnp.zeros((8, 128), jnp.int32).at[0, :slot_count].set(ids)
-    info = info.at[1, :passages_here].set(valid_len)
-    table, infos = gather_all(encoded.reshape(passages_here * passage_len, width), info, n)
-
-    all_ids = infos[:, 0, :slot_count]
+    table, infos = gather_all(
+        encoded.reshape(passages_here * passage_len, width),
+        retrieved,
+        valid_len.reshape(1, passages_here),
+        n,
+    )
+    all_ids = infos[:, :questions_here, :per_question].reshape(n, slot_count)
     attended, d_decoder, slots, grads = attend_all(
-        ids,
+        retrieved,
         infos,
         decoder_states.reshape(questions_here * dec_len, width),
         cotangent.reshape(questions_here * dec_len, width),

time: 234 us -> 208 us (0.89); the launches traced: 230 us -> 208 us
  Pallas kernels: 217 us -> 199 us
  local copies, waits for them, and re-layouts: 5.94 us -> 2.63 us
    pallas_call x1, Pallas kernels: 87.1 us -> 74.5 us  [gather_all(): pl.pallas_call(functools.partial(gather_kernel, n, cuts), out_shape=(jax....]
    pallas_call x1, Pallas kernels: 94.3 us -> 88.9 us  [return_all(): pl.pallas_call(functools.partial(return_kernel, n), out_shape=(jax.ShapeD...]
where the time goes in v3:
time: 208 us
  Pallas kernels  199 us (96%)
  matrix products  4.83 us (2%)
  local copies, waits for them, and re-layouts  2.63 us (1%)
    pallas_call x1, Pallas kernels, return_all(): pl.pallas_call(functools.partial(return_kernel, n), out_shape=(jax.ShapeD...  88.9 us
    pallas_call x1, Pallas kernels, gather_all(): pl.pallas_call(functools.partial(gather_kernel, n, cuts), out_shape=(jax....  74.5 us
    pallas_call x1, Pallas kernels, attend_all(): pl.pallas_call(functools.partial(attend_kernel, n, cap, table.shape[0] //...  36 us
    dot_general x1, matrix products, body(): jnp.dot(select, got.reshape(n * cap * passage_len, width), preferred_elem...  4.7 us

profile of v3, /device:TPU:0, one launch (start us, length us, event | category | flops | bytes accessed | tf_op | source)
XLA Modules:
  0.0 207.9 jit_solution(3036960562239000872)
XLA Ops:
  0.6 74.5 %gather_passages.1 = (bf16[16,512,768]{2,1,0:T(8,128)(2,1)}, s32[16,8,128]{2,1,0:T(8,128)}) custom-call(bf16[512,768]{1,0:T(8,128)(2,1)} %bitcast.23, s32[4,16]{1,0:T(4,128)} %ids_ref.3, s32[1,32]{1,0:T(1,128)} %bitcast.26), custom_call_target="tpu_custom_call" | custom-call | tf_op jit(solution)/shard_map/gather_passages/pallas_call | solution.py:186
  75.1 36.0 %attend.1 = (bf16[256,768]{1,0:T(8,128)(2,1)}, bf16[256,768]{1,0:T(8,128)(2,1)}, bf16[128,16,768]{2,1,0:T(8,128)(2,1)}, bf16[2,2,4,4,48,768]{5,4,3,2,1,0:T(8,128)(2,1)}) custom-call(s32[4,16]{1,0:T(4,128)} %ids_ref.3, s32[16,8,128]{2,1,0:T(8,128)} %get-tuple-element.15.infos_ref, bf16[256,768]{1,0:T(8,128)(2,1)} %bitcast.24, bf16[256,768]{1,0:T(8,128)(2,1)} %bitcast.25, ...), custom_call_target="tpu_custom_call" | custom-call | tf_op jit(solution)/shard_map/attend/pallas_call | solution.py:469
  111.1 0.0 copy-start.1
  111.1 88.9 %return_gradients.1 = (bf16[16,128,768]{2,1,0:T(8,128)(2,1)S(1)}, f32[4,48,768]{2,1,0:T(8,128)S(1)}) custom-call(bf16[16,128,768]{2,1,0:T(8,128)(2,1)} %bitcast.22, bf16[2,2,4,4,48,768]{5,4,3,2,1,0:T(8,128)(2,1)} %get-tuple-element.20.g_ref), custom_call_target="tpu_custom_call" | custom-call | tf_op jit(solution)/shard_map/return_gradients/pallas_call | solution.py:301
  200.0 0.0 copy-start
  200.0 1.6 copy-done
  201.6 0.0 copy-done.1
  201.6 0.1 reshape.110
  201.8 0.1 fusion.4
  201.9 0.4 select_reduce_fusion
  202.3 0.1 iota_add_fusion
  202.3 0.1 add.43
  202.4 4.7 %fusion.2 = bf16[512,768]{1,0:T(8,128)(2,1)} fusion(bf16[2048,768]{1,0:T(8,128)(2,1)} %bitcast.20, s32[2048]{0:T(1024)S(1)} %compare_select_fusion), kind=kOutput, calls=%fused_computation.3 | convolution fusion | flops 1612054528 | bytes 3940352 | tf_op jit(solution)/shard_map/dot_general | solution.py:544
  207.1 0.8 slice_bitcast_fusion
  (5 shorter events, 0.0 us)
Async XLA Ops:
  111.1 90.5 %copy-start.1 = (s32[16,8,128]{2,1,0:T(8,128)S(1)}, s32[16,8,128]{2,1,0:T(8,128)}, u32[]{:S(2)}) copy-start(s32[16,8,128]{2,1,0:T(8,128)} %get-tuple-element.15.infos_ref) | copy-start | bytes 196612
  200.0 1.6 copy-start

commit v4 on v3

--- a/solution.py
+++ b/solution.py
@@ -223,11 +223,17 @@
     first = remote(g_ref.at[1 - c], r1, sem1.at[0], sem1.at[1], sibling)
     first.start()
     slot_copies = []
-    for k in range(1, n):
-        target = lax.rem(me + k, n)
-        copy = remote(slots_ref.at[target], got_ref.at[me], send_a.at[k], recv_a.at[me], target)
+
+    def ship(target):
+        copy = remote(slots_ref.at[target], got_ref.at[me], send_a.at[target], recv_a.at[me], target)
         copy.start()
         slot_copies.append(copy)
+
+    shifts = sorted(range(1, depth), key=lambda k: abs(2 * k - depth))
+    for k in shifts:
+        for core in (c, 1 - c):
+            ship(index_of(lax.rem(z + k, depth), y, core))
+    ship(sibling)
     own = pltpu.make_async_copy(slots_ref.at[me], got_ref.at[me], own_sem)
     own.start()
     first.wait()
@@ -240,6 +246,9 @@
     lax.fori_loop(0, depth, add1, 0)
     second = remote(s1.at[1 - y], r2, sem2.at[0], sem2.at[1], across)
     second.start()
+    for k in shifts + [0]:
+        for core in (c, 1 - c):
+            ship(index_of(lax.rem(z + k, depth), 1 - y, core))
     second.wait()
 
     def add2(i, carry):
@@ -289,7 +298,7 @@
     for k in range(1, n):
         slot_copies[k - 1].wait_send()
         source = lax.rem(me + n - k, n)
-        remote(slots_ref.at[source], got_ref.at[source], send_a.at[k], recv_a.at[source], source).wait_recv()
+        remote(slots_ref.at[source], got_ref.at[source], send_a.at[source], recv_a.at[source], source).wait_recv()
     own.wait()
 
 
@@ -409,8 +418,9 @@
             zero = jnp.zeros_like(qp)
             q2 = jnp.concatenate([jnp.where(low, qp, zero), jnp.where(low, zero, qp)], axis=0)
             c2 = jnp.concatenate([jnp.where(low, cp, zero), jnp.where(low, zero, cp)], axis=0)
+            q2 = q2 * jnp.asarray(scale, BF)
             kp, vp = keys[kat, cols], values[kat, cols]
-            scores = nt(kp, q2) * scale + dead
+            scores = nt(kp, q2) + dead
             top = jnp.max(scores, axis=0, keepdims=True)
             expo = jnp.exp(scores - top)
             probs = expo * (1.0 / jnp.sum(expo, axis=0, keepdims=True))
@@ -420,8 +430,8 @@
             vg[kat, cols] = nn(probs_b, c2).astype(BF)
             pgrad = nt(vp, c2)
             inner = jnp.sum(probs * pgrad, axis=0, keepdims=True)
-            sgrad = (probs * (pgrad - inner) * scale).astype(BF)
-            both_q = tn(sgrad, kp)
+            sgrad = (probs * (pgrad - inner)).astype(BF)
+            both_q = tn(sgrad, kp) * scale
             qg[tat, cols] = jnp.where(low, both_q[:tokens], both_q[tokens:]).astype(BF)
             kg[kat, cols] = nn(sgrad, q2).astype(BF)
         return carry

time: 208 us -> 208 us (level)
  no operation moved by 1% of the time
where the time goes in v4:
time: 208 us; the launch traced here: 207 us
  Pallas kernels  199 us (96%)
  matrix products  4.83 us (2%)
  local copies, waits for them, and re-layouts  2.63 us (1%)
    pallas_call x1, Pallas kernels, return_all(): pl.pallas_call(functools.partial(return_kernel, n), out_shape=(jax.ShapeD...  88.4 us
    pallas_call x1, Pallas kernels, gather_all(): pl.pallas_call(functools.partial(gather_kernel, n, cuts), out_shape=(jax....  74.5 us
    pallas_call x1, Pallas kernels, attend_all(): pl.pallas_call(functools.partial(attend_kernel, n, cap, table.shape[0] //...  35.9 us
    dot_general x1, matrix products, body(): jnp.dot(select, got.reshape(n * cap * passage_len, width), preferred_elem...  4.7 us

profile of v4, /device:TPU:0, one launch (start us, length us, event | category | flops | bytes accessed | tf_op | source)
XLA Modules:
  0.0 207.4 jit_solution(18314476638378722276)
XLA Ops:
  0.6 74.5 %gather_passages.1 = (bf16[16,512,768]{2,1,0:T(8,128)(2,1)}, s32[16,8,128]{2,1,0:T(8,128)}) custom-call(bf16[512,768]{1,0:T(8,128)(2,1)} %bitcast.23, s32[4,16]{1,0:T(4,128)} %ids_ref.3, s32[1,32]{1,0:T(1,128)} %bitcast.26), custom_call_target="tpu_custom_call" | custom-call | tf_op jit(solution)/shard_map/gather_passages/pallas_call | solution.py:186
  75.1 35.9 %attend.1 = (bf16[256,768]{1,0:T(8,128)(2,1)}, bf16[256,768]{1,0:T(8,128)(2,1)}, bf16[128,16,768]{2,1,0:T(8,128)(2,1)}, bf16[2,2,4,4,48,768]{5,4,3,2,1,0:T(8,128)(2,1)}) custom-call(s32[4,16]{1,0:T(4,128)} %ids_ref.3, s32[16,8,128]{2,1,0:T(8,128)} %get-tuple-element.15.infos_ref, bf16[256,768]{1,0:T(8,128)(2,1)} %bitcast.24, bf16[256,768]{1,0:T(8,128)(2,1)} %bitcast.25, ...), custom_call_target="tpu_custom_call" | custom-call | tf_op jit(solution)/shard_map/attend/pallas_call | solution.py:479
  111.0 0.0 copy-start.1
  111.0 88.4 %return_gradients.1 = (bf16[16,128,768]{2,1,0:T(8,128)(2,1)S(1)}, f32[4,48,768]{2,1,0:T(8,128)S(1)}) custom-call(bf16[16,128,768]{2,1,0:T(8,128)(2,1)} %bitcast.22, bf16[2,2,4,4,48,768]{5,4,3,2,1,0:T(8,128)(2,1)} %get-tuple-element.20.g_ref), custom_call_target="tpu_custom_call" | custom-call | tf_op jit(solution)/shard_map/return_gradients/pallas_call | solution.py:310
  199.5 0.0 copy-start
  199.5 1.6 copy-done
  201.1 0.0 copy-done.1
  201.1 0.1 reshape.110
  201.2 0.1 fusion.4
  201.4 0.4 select_reduce_fusion
  201.7 0.1 iota_add_fusion
  201.8 0.1 add.43
  201.9 4.7 %fusion.2 = bf16[512,768]{1,0:T(8,128)(2,1)} fusion(bf16[2048,768]{1,0:T(8,128)(2,1)} %bitcast.20, s32[2048]{0:T(1024)S(1)} %compare_select_fusion), kind=kOutput, calls=%fused_computation.3 | convolution fusion | flops 1612054528 | bytes 3940352 | tf_op jit(solution)/shard_map/dot_general | solution.py:554
  206.6 0.8 slice_bitcast_fusion
  (5 shorter events, 0.0 us)
Async XLA Ops:
  111.0 90.1 %copy-start.1 = (s32[16,8,128]{2,1,0:T(8,128)S(1)}, s32[16,8,128]{2,1,0:T(8,128)}, u32[]{:S(2)}) copy-start(s32[16,8,128]{2,1,0:T(8,128)} %get-tuple-element.15.infos_ref) | copy-start | bytes 196612
  199.5 1.6 copy-start
